TPU v7x, 128 devices: a whole 4x4x4 slice. The times are simulated.
128 devices in a mesh: mem: 8 (over z_lo, y), tile: 16 (over x, z_hi, core).
Axes of the slice: x: 4, y: 4, z: 4 (z_hi: 2, z_lo: 2; z = z_hi * 2 + z_lo), core: 2. Of those that a mesh axis runs over, the one named last changes fastest.
Arguments:
- hidden_in: bfloat16 [32, 4096, 1024], P('mem', 'tile'), may hold values from -6 to 6
- norm_gain: bfloat16 [1024], replicated, may hold values from 0.5 to 1.5
- w_in: bfloat16 [1024, 4096], replicated, may hold values from -0.1875 to 0.1875
- w_out: bfloat16 [4096, 1024], replicated, may hold values from -0.09375 to 0.09375
- w_dec: bfloat16 [69, 1024], replicated, may hold values from -0.1875 to 0.1875
- observed: float32 [69, 256, 16], P(None, 'tile'), may hold values from -16 to 16
- obs_count: int32 [69, 256, 16], P(None, 'tile'), may hold values from 0 to 3, as said below
- obs_error: float32 [69], replicated, may hold values from 2 to 6
Outputs:
- increments: float32 [32, 69, 16, 256], P('mem', None, 'tile')
Inputs may be any that keep to these rules, and one draw needn't show every extreme that they name: `obs_count`: each entry is 0 or 3 and is the same for all variables at a grid point; it is 3 exactly where one of 5 observed latitude rows meets one of 192 observed longitude columns.
All inputs are finite; a program needn't handle non-finite values.
Results may differ from a plain program's by a relative error of at most 0.02.
Values may be sent and summed in bfloat16 or wider, within the bound.
No kernel may reach another device: no remote copies, remote signals or barrier semaphores. Data moves between devices by JAX's collectives and lax.ppermute only.
A program may use at most 128 MiB of HBM per device.

v0:
```python
import functools
import math

import jax
import jax.numpy as jnp
import numpy as np
from jax import lax
from jax.experimental import pallas as pl
from jax.experimental.pallas import tpu as pltpu
from jax.sharding import PartitionSpec as P

RAD = 6
NS_ITERS = 4
F32 = jnp.float32
BF16 = jnp.bfloat16

LANES = 128
VROWS = 72
HROWS = 40
HALO = 8
SECTOR = 32
MEMBERS = 32
GROUP = 4
DIAGS = MEMBERS // 2 + 1
ROWS = DIAGS + 1
FF_BLOCK = 1024
TOKEN_BLOCK = 512

VMEM = pltpu.CompilerParams(vmem_limit_bytes=60 * 2**20)


def lanes_of(shape):
    return lax.broadcasted_iota(jnp.int32, shape, len(shape) - 1)


def gelu(h):
    inner = h * (math.sqrt(2.0 / math.pi) + (0.044715 * math.sqrt(2.0 / math.pi)) * (h * h))
    half = 0.5 * h
    return half + half * jnp.tanh(inner)


def forecast_kernel(x_ref, gain_ref, win_ref, wout_ref, wdec_ref, out_ref, normed, acc):
    step = pl.program_id(0)
    steps = pl.num_programs(0)
    tokens = x_ref.shape[0]
    blocks = tokens // TOKEN_BLOCK
    lon_all = tokens // GROUP

    @pl.when(step == 0)
    def _():
        gain = gain_ref[...].astype(F32)
        for r in range(tokens // 128):
            xf = x_ref[pl.ds(r * 128, 128), :].astype(F32)
            centred = xf - jnp.mean(xf, axis=-1, keepdims=True)
            spread = jnp.mean(centred * centred, axis=-1, keepdims=True)
            normed[pl.ds(r * 128, 128), :] = (centred * lax.rsqrt(spread + 1e-05) * gain).astype(BF16)

    def up(r):
        return jnp.dot(
            normed[pl.ds(r * TOKEN_BLOCK, TOKEN_BLOCK), :], win_ref[...], preferred_element_type=F32
        )

    def run(first):
        hidden = up(0)
        for r in range(blocks):
            following = up(r + 1) if r + 1 < blocks else None
            down = jnp.dot(gelu(hidden).astype(BF16), wout_ref[...], preferred_element_type=F32)
            at = pl.ds(r * TOKEN_BLOCK, TOKEN_BLOCK)
            if first:
                acc[at, :] = down
            else:
                acc[at, :] += down
            hidden = following

    @pl.when(step == 0)
    def _():
        run(True)

    @pl.when(step > 0)
    def _():
        run(False)

    @pl.when(step == steps - 1)
    def _():
        acc[...] = x_ref[...].astype(F32) + acc[...]
        wdec = wdec_ref[...]
        contract = (((1,), (1,)), ((), ()))
        for i in range(lon_all // SECTOR):
            main, halo = [], []
            for m in range(GROUP):
                base = m * lon_all
                main.append(acc[pl.ds(base + SECTOR * i, SECTOR), :])
                halo.append(acc[pl.ds(base + (SECTOR * i - HALO) % lon_all, HALO), :])
                halo.append(acc[pl.ds(base + (SECTOR * (i + 1)) % lon_all, HALO), :])
            main = jnp.concatenate(main, axis=0).astype(BF16)
            halo = jnp.concatenate(halo, axis=0).astype(BF16)
            main = lax.dot_general(wdec, main, contract, preferred_element_type=F32)
            halo = lax.dot_general(wdec, halo, contract, preferred_element_type=F32)
            halo = jnp.concatenate([halo[:HROWS], halo[HROWS:]], axis=1)
            out_ref[i] = jnp.concatenate([main[:VROWS], halo], axis=0).astype(BF16)


def forecast(x, gain, w_in, w_out, w_dec):
    tokens, width = x.shape
    hidden = w_in.shape[1]
    sectors = tokens // GROUP // SECTOR
    return pl.pallas_call(
        forecast_kernel,
        grid=(hidden // FF_BLOCK,),
        in_specs=[
            pl.BlockSpec((tokens, width), lambda s: (0, 0)),
            pl.BlockSpec((1, width), lambda s: (0, 0)),
            pl.BlockSpec((width, FF_BLOCK), lambda s: (0, s)),
            pl.BlockSpec((FF_BLOCK, width), lambda s: (s, 0)),
            pl.BlockSpec((2 * HROWS, width), lambda s: (0, 0)),
        ],
        out_specs=pl.BlockSpec((sectors, VROWS + HROWS, LANES), lambda s: (0, 0, 0)),
        out_shape=jax.ShapeDtypeStruct((sectors, VROWS + HROWS, LANES), BF16),
        scratch_shapes=[pltpu.VMEM((tokens, width), BF16), pltpu.VMEM((tokens, width), F32)],
        compiler_params=VMEM,
        cost_estimate=pl.CostEstimate(
            flops=4 * tokens * width * hidden, bytes_accessed=4 * width * hidden, transcendentals=0
        ),
        name="forecast",
    )(x, gain, w_in, w_out, w_dec)


def copies_over_lanes(tile, width):
    while width < LANES:
        tile = tile + pltpu.roll(tile, width, 1)
        width *= 2
    return tile


def sum_over_groups(tile, width):
    while width < LANES:
        tile = tile + pltpu.roll(tile, width, 1)
        width *= 2
    return tile


def shifted_tile(tiles, index, shift, width):
    move = shift * width
    if not move:
        return tiles(index)
    here = pltpu.roll(tiles(index), LANES - move, 1)
    there = pltpu.roll(tiles(index + 1), LANES - move, 1)
    return jnp.where(lanes_of(here.shape) < LANES - move, here, there)


def pair_sums(fields, observed, inv_count, width, weighted, moved, anomalies, put):
    count = len(fields)
    per = LANES // width
    total = fields[0]
    for tile in fields[1:]:
        total = total + tile
    mean = sum_over_groups(total, width) / MEMBERS
    for k in range(count):
        anomaly = fields[k] - mean
        if anomalies is not None:
            anomalies[k] = anomaly
        weighted[k] = (anomaly * inv_count).astype(BF16).astype(F32)
        moved[0, k] = anomaly.astype(BF16).astype(F32)
    for t in range(1, per):
        for k in range(count):
            moved[t, k] = shifted_tile(lambda j: moved[0, j % count], k, t, width)
    innovation = observed - mean
    for k in range(count):
        put(DIAGS, k, jnp.sum(weighted[k] * innovation, axis=0, keepdims=True))
    for s in range(DIAGS):
        on, t = divmod(s, per)
        for k in range(count):
            put(s, k, jnp.sum(weighted[k] * moved[t, (k + on) % count], axis=0, keepdims=True))


def pairs_kernel(
    place_ref, recv_ref, obs_ref, err_ref, taper_ref, out_ref, anom_ref,
    weighted, moved, weighted_halo, moved_halo, sums,
):
    tiles = recv_ref.shape[0]
    lon_all = obs_ref.shape[1]
    obs = pltpu.roll(obs_ref[...], lax.rem(lon_all - SECTOR * place_ref[0], lon_all), 1)
    first, last = obs[:, :LANES], obs[:, lon_all - LANES :]
    lane = lanes_of(first.shape)
    obs_main = copies_over_lanes(jnp.where(lane < SECTOR, first, 0.0), SECTOR)
    obs_halo = jnp.where(
        lane < HALO,
        pltpu.roll(last, HALO, 1),
        jnp.where(lane < 2 * HALO, pltpu.roll(first, LANES - SECTOR + HALO, 1), 0.0),
    )
    obs_halo = copies_over_lanes(obs_halo, 2 * HALO)
    variables = VROWS - 3
    err = err_ref[...]
    prec_main = obs_main[variables : variables + 1] / (err * err)
    prec_halo = obs_halo[variables : variables + 1] / (err * err)

    sums[...] = jnp.zeros_like(sums)

    def put_main(s, k, row):
        sums[pl.ds(s * tiles + k, 1), 0:LANES] = row

    def put_halo(s, k, row):
        sums[pl.ds(s * tiles + 2 * k, 1), LANES : 2 * LANES] = row
        sums[pl.ds(s * tiles + 2 * k + 1, 1), 2 * LANES : 3 * LANES] = row

    fields, halos = [], []
    for m in range(tiles):
        both = recv_ref[m].astype(F32)
        fields.append(both[:VROWS])
        halos.append(both[VROWS:])
    left = lanes_of((HROWS, LANES)) < LANES // 2
    halo_fields = []
    for h in range(tiles // 2):
        a, b = halos[2 * h], halos[2 * h + 1]
        upper = jnp.where(left, a, pltpu.roll(b, LANES // 2, 1))
        lower = jnp.where(left, pltpu.roll(a, LANES // 2, 1), b)
        halo_fields.append(jnp.concatenate([upper, lower], axis=0)[:VROWS])
    pair_sums(fields, obs_main, prec_main, SECTOR, weighted, moved, anom_ref, put_main)
    pair_sums(halo_fields, obs_halo, prec_halo, 2 * HALO, weighted_halo, moved_halo, None, put_halo)
    smooth = jnp.dot(
        sums[...], taper_ref[...], precision=lax.Precision.HIGHEST, preferred_element_type=F32
    ).astype(BF16)
    for a in range(out_ref.shape[0]):
        out_ref[a] = smooth


def taper_of(offset):
    offset = np.asarray(offset, np.float32)
    ratio = offset / np.float32(RAD + 1.0)
    return np.where(np.abs(offset) <= RAD, (1.0 - ratio * ratio) ** 2, 0.0).astype(np.float32)


def longitude_taper():
    out_member, out_col = np.divmod(np.arange(LANES), SECTOR)
    main_member, main_col = np.divmod(np.arange(LANES), SECTOR)
    halo_member, halo_place = np.divmod(np.arange(LANES), 2 * HALO)
    halo_col = np.where(halo_place < HALO, halo_place - HALO, halo_place - HALO + SECTOR)
    parts = []
    for member, col in (
        (main_member, main_col), (halo_member, halo_col), (halo_member - GROUP, halo_col)
    ):
        same = member[:, None] == out_member[None, :]
        parts.append(np.where(same, taper_of(col[:, None] - out_col[None, :]), 0.0))
    return jnp.asarray(np.concatenate(parts, axis=0).astype(np.float32))


def pairs(place, recv, obs, err, n_rows):
    tiles = recv.shape[0]
    full = pl.BlockSpec(memory_space=pltpu.VMEM)
    return pl.pallas_call(
        pairs_kernel,
        in_specs=[pl.BlockSpec(memory_space=pltpu.SMEM), full, full, full, full],
        out_specs=(full, full),
        out_shape=(
            jax.ShapeDtypeStruct((n_rows, ROWS * tiles, LANES), BF16),
            jax.ShapeDtypeStruct((tiles, VROWS, LANES), F32),
        ),
        scratch_shapes=[
            pltpu.VMEM((tiles, VROWS, LANES), F32),
            pltpu.VMEM((LANES // SECTOR, tiles, VROWS, LANES), F32),
            pltpu.VMEM((tiles // 2, VROWS, LANES), F32),
            pltpu.VMEM((LANES // (2 * HALO), tiles // 2, VROWS, LANES), F32),
            pltpu.VMEM((ROWS * tiles, 3 * LANES), F32),
        ],
        compiler_params=VMEM,
        name="pairs",
    )(place, recv, obs, err, longitude_taper())


def on_by(x, n):
    sub, t = divmod(n % MEMBERS, GROUP)
    if t:
        move = LANES - SECTOR * t
        x = pltpu.roll(x, move, 1)
        x = jnp.where(lanes_of(x.shape) < move, x, pltpu.roll(x, 7, 0))
    if sub:
        x = pltpu.roll(x, 8 - sub, 0)
    return x


def shifted_sum(term):
    total = None
    for t in range(GROUP - 1, -1, -1):
        inner = None
        for a in range(MEMBERS // GROUP - 1, -1, -1):
            part = term(GROUP * a + t)
            inner = part if inner is None else on_by(inner, GROUP) + part
        total = inner if total is None else on_by(total, 1) + inner
    return total


def product(left, right, out, scale=None, shift=None):
    for s in range(DIAGS):
        value = shifted_sum(lambda t: left[(-t) % MEMBERS] * right[(s - t) % MEMBERS])
        if scale is not None:
            value = scale * value
            if s == 0:
                value = value + shift
        out[s] = value
    mirror(out)


def mirror(out):
    for s in range(1, MEMBERS - DIAGS + 1):
        out[MEMBERS - s] = on_by(out[s], -s)


def transform_kernel(lat_ref, recv_ref, anom_ref, out_ref, bank, moved, coeff):
    rows = recv_ref.shape[0]
    tiles = anom_ref.shape[0]
    local = lat_ref[0] * recv_ref[0].astype(F32)
    for b in range(1, rows):
        local = local + lat_ref[b] * recv_ref[b].astype(F32)
    diag = [local[s * tiles : (s + 1) * tiles] for s in range(ROWS)]
    innov = diag[DIAGS]
    diag[0] = diag[0] + (MEMBERS - 1.0)
    gram, root, inv_root, corr = bank.at[0], bank.at[1], bank.at[2], bank.at[3]
    other_root, other_inv = bank.at[4], bank.at[5]
    square = None
    for s in range(DIAGS):
        part = diag[s] * diag[s]
        if 0 < s < DIAGS - 1:
            part = part + part
        square = part if square is None else square + part
    square = jnp.broadcast_to(jnp.sum(square, axis=0, keepdims=True), square.shape)
    frob = jnp.sqrt(sum_over_groups(square, SECTOR))
    inv_frob = 1.0 / frob
    for s in range(DIAGS):
        gram[s] = diag[s] * inv_frob
    mirror(gram)
    for s in range(MEMBERS):
        inv_root[s] = -0.5 * gram[s] + (1.5 if s == 0 else 0.0)
    product(gram, inv_root, root)
    for sweep in range(1, NS_ITERS):
        product(inv_root, root, corr, -0.5, 1.5)
        if sweep < NS_ITERS - 1:
            product(root, corr, other_root)
        product(corr, inv_root, other_inv)
        root, other_root = other_root, root
        inv_root, other_inv = other_inv, inv_root
    half = shifted_sum(lambda t: inv_root[(-t) % MEMBERS] * innov)
    mean_weights = shifted_sum(lambda t: inv_root[(-t) % MEMBERS] * half) * inv_frob
    factor = math.sqrt(MEMBERS - 1.0) / jnp.sqrt(frob)
    for s in range(MEMBERS):
        value = inv_root[s] * factor + on_by(mean_weights, s)
        coeff[pl.ds(s * tiles, tiles), :] = value.astype(BF16).astype(F32)
    for k in range(tiles):
        moved[0, k] = anom_ref[k].astype(BF16).astype(F32)
    for t in range(1, GROUP):
        for k in range(tiles):
            moved[t, k] = shifted_tile(lambda j: moved[0, j % tiles], k, t, SECTOR)
    for k in range(tiles):
        mixed = None
        for s in range(MEMBERS):
            on, t = divmod(s, GROUP)
            part = moved[t, (k + on) % tiles] * coeff[pl.ds(s * tiles + k, 1), :]
            mixed = part if mixed is None else mixed + part
        out_ref[k] = (mixed - anom_ref[k]).astype(BF16)


def transform(lat_taper, recv, anomaly):
    tiles = anomaly.shape[0]
    full = pl.BlockSpec(memory_space=pltpu.VMEM)
    return pl.pallas_call(
        transform_kernel,
        in_specs=[pl.BlockSpec(memory_space=pltpu.SMEM), full, full],
        out_specs=full,
        out_shape=jax.ShapeDtypeStruct((tiles, VROWS, LANES), BF16),
        scratch_shapes=[
            pltpu.VMEM((6, MEMBERS, tiles, LANES), F32),
            pltpu.VMEM((GROUP, tiles, VROWS, LANES), F32),
            pltpu.VMEM((MEMBERS * tiles, LANES), F32),
        ],
        compiler_params=VMEM,
        name="transform",
    )(lat_taper, recv, anomaly)


def strips_kernel(recv_ref, out_ref):
    tiles = recv_ref.shape[0]
    variables = out_ref.shape[1]
    parts = [recv_ref[i].astype(F32) for i in range(tiles)]
    group = lanes_of(parts[0].shape) // SECTOR
    for m in range(GROUP):
        for c in range(tiles // GROUP):
            tile = None
            for j in range(GROUP):
                piece = parts[GROUP * c + j]
                if j != m:
                    piece = pltpu.roll(piece, (SECTOR * (j - m)) % LANES, 1)
                tile = piece if tile is None else jnp.where(group == j, piece, tile)
            out_ref[m, :, pl.ds(c * LANES, LANES)] = tile[:variables]


def strips(recv, variables):
    tiles = recv.shape[0]
    full = pl.BlockSpec(memory_space=pltpu.VMEM)
    return pl.pallas_call(
        strips_kernel,
        in_specs=[full],
        out_specs=full,
        out_shape=jax.ShapeDtypeStruct((GROUP, variables, tiles * SECTOR), F32),
        compiler_params=VMEM,
        name="strips",
    )(recv)


def body(hidden_in, norm_gain, w_in, w_out, w_dec, observed, obs_count, obs_error):
    mem_dev, tok_dev, width = hidden_in.shape
    variables, lon_dev, lat_all = observed.shape
    lon_all = lon_dev * lax.axis_size("tile")
    place = lax.axis_index("mem").astype(jnp.int32).reshape(1)
    lat_ids = jnp.arange(lat_all, dtype=jnp.int32) - lax.axis_index("tile")
    ratio = lat_ids.astype(F32) / (RAD + 1.0)
    lat_taper = jnp.where(jnp.abs(lat_ids) <= RAD, (1.0 - ratio * ratio) ** 2, 0.0)

    obs = jnp.concatenate([observed, obs_count[:1].astype(F32)], axis=0)
    obs = lax.all_to_all(obs, "tile", split_axis=2, concat_axis=1, tiled=True)
    obs = jnp.pad(obs.reshape(variables + 1, lon_all), ((0, VROWS - variables - 1), (0, 0)))
    err = jnp.pad(obs_error, (0, VROWS - variables), constant_values=1.0).reshape(VROWS, 1)

    fields = forecast(
        hidden_in.reshape(mem_dev * tok_dev, width),
        norm_gain.reshape(1, width),
        w_in,
        w_out,
        jnp.pad(w_dec, ((0, 2 * HROWS - variables), (0, 0))),
    )
    sectors = lax.all_to_all(fields, "mem", 0, 0, tiled=True)
    smooth, anomaly = pairs(place, sectors, obs, err, lat_all)
    rows = lax.all_to_all(smooth, "tile", 0, 0, tiled=True)
    increments = transform(lat_taper, rows, anomaly)
    back = lax.all_to_all(increments, "mem", 0, 0, tiled=True)
    return strips(back, variables).reshape(mem_dev, variables, tok_dev // lon_all, lon_all)


def solution(mesh):
    return jax.shard_map(
        body,
        mesh=mesh,
        in_specs=(
            P("mem", "tile", None),
            P(),
            P(),
            P(),
            P(),
            P(None, "tile", None),
            P(None, "tile", None),
            P(),
        ),
        out_specs=P("mem", None, "tile", None),
        check_vma=False,
    )
```

profile of v0, /device:TPU:1, one launch (start us, length us, event | category | flops | bytes accessed | tf_op | source)
XLA Modules:
  0.0 96.2 jit_solution(3581884584892911664)
XLA Ops:
  0.0 0.9 copy.18
  1.0 1.0 copy_convert_fusion
  1.9 0.8 pad_maximum_fusion
  2.7 9.1 %all-to-all-start.1 = ((f32[70,16,16]{0,1,2:T(8,128)}), f32[70,16,16]{0,1,2:T(8,128)S(1)}, u32[]{:S(2)}, u32[]{:S(2)}) async-start(f32[70,16,16]{0,1,2:T(8,128)} %pad_maximum_fusion), calls=%async_computation.1 | async-start | bytes 262144 | tf_op jit(solution)/shard_map/all_to_all | solution.py:418
  11.8 1.3 %reshape.21.gain_ref = bf16[1,1024]{1,0:T(2,128)(2,1)} reshape(bf16[1024]{0:T(1024)(128)(2,1)} %param.10) | data formatting | bytes 4096 | tf_op jit(solution)/shard_map/reshape | solution.py:424
  13.1 1.6 %pad.12.wdec_ref = bf16[80,1024]{1,0:T(8,128)(2,1)} pad(bf16[69,1024]{1,0:T(8,128)(2,1)} %param.13, bf16[]{:T(256)} %constant.24.clone.1), padding=0_11x0_0 | pad | bytes 305154 | tf_op jit(solution)/shard_map/jit(_pad)/pad | solution.py:427
  14.6 0.0 copy-start.2
  14.6 24.9 %forecast.1 = bf16[8,112,128]{2,1,0:T(8,128)(2,1)} custom-call(bf16[1024,1024]{1,0:T(8,128)(2,1)} %bitcast.14, bf16[1,1024]{1,0:T(2,128)(2,1)} %reshape.21.gain_ref, bf16[1024,4096]{1,0:T(8,128)(2,1)} %win_ref.1, bf16[4096,1024]{1,0:T(8,128)(2,1)} %wout_ref.1, bf16[80,1024]{1,0:T(8,128)(2,1)} %pad.12.wdec_ref), custom_call_target="tpu_custom_call" | custom-call | flops 17179869184 | bytes 16777216 | tf_op jit(solution)/shard_map/forecast/pallas_call | solution.py:107
  39.6 0.0 all-to-all-done.1
  39.6 4.6 %all-to-all-start = ((bf16[8,112,128]{2,1,0:T(8,128)(2,1)}), bf16[8,112,128]{2,1,0:T(8,128)(2,1)S(1)}, u32[]{:S(2)}, u32[]{:S(2)}) async-start(bf16[8,112,128]{2,1,0:T(8,128)(2,1)} %forecast.1), calls=%async_computation | async-start | bytes 458752 | tf_op jit(solution)/shard_map/all_to_all | solution.py:429
  44.2 0.0 copy-done.2
  44.3 0.7 copy.20.err_ref
  45.0 0.1 copy.19
  45.1 0.7 pad.13.obs_ref
  45.7 5.4 %all-to-all-done.recv_ref = bf16[8,112,128]{2,1,0:T(8,128)(2,1)S(1)} async-done(((bf16[8,112,128]{2,1,0:T(8,128)(2,1)}), bf16[8,112,128]{2,1,0:T(8,128)(2,1)S(1)}, u32[]{:S(2)}, u32[]{:S(2)}) %all-to-all-start) | async-done | bytes 229408 | tf_op jit(solution)/shard_map/all_to_all | solution.py:429
  51.1 0.0 copy-start.1
  51.1 0.7 copy-done.1
  51.8 3.7 %pairs.1 = (bf16[16,144,128]{2,1,0:T(8,128)(2,1)}, f32[8,72,128]{2,1,0:T(8,128)}) custom-call(s32[1]{0:T(128)} %bitcast.place_ref, bf16[8,112,128]{2,1,0:T(8,128)(2,1)} %copy-done.1, f32[72,256]{1,0:T(8,128)} %pad.13.obs_ref, f32[72,1]{1,0:T(8,128)} %copy.20.err_ref, f32[384,128]{1,0:T(8,128)} %constant.25.clone.taper_ref), custom_call_target="tpu_custom_call" | custom-call | tf_op jit(solution)/shard_map/pairs/pallas_call | solution.py:250
  55.5 8.6 %all-to-all-start.2 = ((bf16[16,144,128]{2,1,0:T(8,128)(2,1)}), bf16[16,144,128]{2,1,0:T(8,128)(2,1)S(1)}, u32[]{:S(2)}, u32[]{:S(2)}) async-start(bf16[16,144,128]{2,1,0:T(8,128)(2,1)} %get-tuple-element.7), calls=%async_computation.2 | async-start | bytes 1179648 | tf_op jit(solution)/shard_map/all_to_all | solution.py:431
  64.1 0.6 compare_select_fusion.lat_ref
  64.7 11.1 %all-to-all-done.2.recv_ref = bf16[16,144,128]{2,1,0:T(8,128)(2,1)S(1)} async-done(((bf16[16,144,128]{2,1,0:T(8,128)(2,1)}), bf16[16,144,128]{2,1,0:T(8,128)(2,1)S(1)}, u32[]{:S(2)}, u32[]{:S(2)}) %all-to-all-start.2) | async-done | bytes 589856 | tf_op jit(solution)/shard_map/all_to_all | solution.py:431
  75.8 0.0 copy-start
  75.8 0.8 copy-done
  76.6 6.3 %transform.1 = bf16[8,72,128]{2,1,0:T(8,128)(2,1)} custom-call(f32[16]{0:T(128)} %compare_select_fusion.lat_ref, bf16[16,144,128]{2,1,0:T(8,128)(2,1)} %copy-done, f32[8,72,128]{2,1,0:T(8,128)} %get-tuple-element.8.anom_ref), custom_call_target="tpu_custom_call" | custom-call | tf_op jit(solution)/shard_map/transform/pallas_call | solution.py:364
  82.9 9.5 %all_to_all.30.recv_ref = bf16[8,72,128]{2,1,0:T(8,128)(2,1)} all-to-all(bf16[8,72,128]{2,1,0:T(8,128)(2,1)} %transform.1), channel_id=1, replica_groups=mesh['mem'=8,'tile'=16] {'mem'}, dimensions={0} | all-to-all | bytes 294912 | tf_op jit(solution)/shard_map/all_to_all | solution.py:433
  92.4 1.8 %strips.1 = f32[4,69,256]{2,1,0:T(8,128)} custom-call(bf16[8,72,128]{2,1,0:T(8,128)(2,1)} %all_to_all.30.recv_ref), custom_call_target="tpu_custom_call" | custom-call | tf_op jit(solution)/shard_map/strips/pallas_call | solution.py:398
  94.2 2.0 %copy.21 = f32[4,69,1,256]{3,2,1,0:T(1,128)} copy(f32[4,69,1,256]{3,1,0,2:T(8,128)} %bitcast.11) | data formatting | bytes 565248 | tf_op jit(solution)/shard_map/reshape | solution.py:434
  (1 shorter events, 0.0 us)
Async XLA Ops:
  2.7 36.9 %all-to-all-start.1 = ((f32[70,16,16]{0,1,2:T(8,128)}), f32[70,16,16]{0,1,2:T(8,128)S(1)}, u32[]{:S(2)}, u32[]{:S(2)}) async-start(f32[70,16,16]{0,1,2:T(8,128)} %pad_maximum_fusion), calls=%async_computation.1 | async-start | bytes 262144 | tf_op jit(solution)/shard_map/all_to_all | solution.py:418
  14.6 29.6 %copy-start.2 = (f32[69]{0:T(128)S(1)}, f32[69]{0:T(128)}, u32[]{:S(2)}) copy-start(f32[69]{0:T(128)} %param.16) | copy-start | bytes 832
  39.6 11.5 %all-to-all-start = ((bf16[8,112,128]{2,1,0:T(8,128)(2,1)}), bf16[8,112,128]{2,1,0:T(8,128)(2,1)S(1)}, u32[]{:S(2)}, u32[]{:S(2)}) async-start(bf16[8,112,128]{2,1,0:T(8,128)(2,1)} %forecast.1), calls=%async_computation | async-start | bytes 458752 | tf_op jit(solution)/shard_map/all_to_all | solution.py:429
  51.1 0.7 copy-start.1
  55.5 20.3 %all-to-all-start.2 = ((bf16[16,144,128]{2,1,0:T(8,128)(2,1)}), bf16[16,144,128]{2,1,0:T(8,128)(2,1)S(1)}, u32[]{:S(2)}, u32[]{:S(2)}) async-start(bf16[16,144,128]{2,1,0:T(8,128)(2,1)} %get-tuple-element.7), calls=%async_computation.2 | async-start | bytes 1179648 | tf_op jit(solution)/shard_map/all_to_all | solution.py:431
  75.8 0.8 copy-start
where the time goes:
time: 98.1 us; the launch traced here: 96.2 us
  Pallas kernels  36.7 us (37%)
  starting transfers between devices  22.4 us (23%)
  waiting for transfers between devices  16.5 us (17%)
  blocking collectives  9.51 us (10%)
  local copies, waits for them, and re-layouts  8.72 us (9%)
  other arithmetic  2.31 us (2%)
    pallas_call x1, Pallas kernels, forecast(): pl.pallas_call(forecast_kernel, grid=(hidden // FF_BLOCK,), in_specs=[pl....  24.9 us
    all_to_all x1, waiting for transfers between devices, body(): rows = lax.all_to_all(smooth, 'tile', 0, 0, tiled=True)  11.1 us
    all_to_all x1, blocking collectives, body(): back = lax.all_to_all(increments, 'mem', 0, 0, tiled=True)  9.51 us
    all_to_all x1, starting transfers between devices, body(): obs = lax.all_to_all(obs, 'tile', split_axis=2, concat_axis=1, tiled=True)  9.13 us
    all_to_all x1, starting transfers between devices, body(): rows = lax.all_to_all(smooth, 'tile', 0, 0, tiled=True)  8.62 us
    pallas_call x1, Pallas kernels, transform(): pl.pallas_call(transform_kernel, in_specs=[pl.BlockSpec(memory_space=pltp...  6.3 us
    all_to_all x1, waiting for transfers between devices, body(): sectors = lax.all_to_all(fields, 'mem', 0, 0, tiled=True)  5.41 us
    all_to_all x1, starting transfers between devices, body(): sectors = lax.all_to_all(fields, 'mem', 0, 0, tiled=True)  4.65 us
  transfers between devices with their start and end apart: 3, of which 2 were waited for; matrix products, arithmetic and copies ran while one was open for 5% of the time, Pallas kernels for 26%

commit v1 on v0

--- a/solution.py
+++ b/solution.py
@@ -26,7 +26,11 @@
 FF_BLOCK = 1024
 TOKEN_BLOCK = 512
 
-VMEM = pltpu.CompilerParams(vmem_limit_bytes=60 * 2**20)
+UNSEEN = 1e30
+COUNT = 3.0
+
+LARGE = pltpu.CompilerParams(vmem_limit_bytes=60 * 2**20)
+SMALL = pltpu.CompilerParams(vmem_limit_bytes=12 * 2**20)
 
 
 def lanes_of(shape):
@@ -39,7 +43,7 @@
     return half + half * jnp.tanh(inner)
 
 
-def forecast_kernel(x_ref, gain_ref, win_ref, wout_ref, wdec_ref, out_ref, normed, acc):
+def forecast_kernel(x_ref, gain_ref, win_ref, wout_ref, wdec_ref, out_ref, normed, acc, decoder):
     step = pl.program_id(0)
     steps = pl.num_programs(0)
     tokens = x_ref.shape[0]
@@ -48,7 +52,9 @@
 
     @pl.when(step == 0)
     def _():
-        gain = gain_ref[...].astype(F32)
+        gain = gain_ref[...].astype(F32).reshape(1, -1)
+        decoder[...] = jnp.zeros_like(decoder)
+        decoder[0 : wdec_ref.shape[0], :] = wdec_ref[...]
         for r in range(tokens // 128):
             xf = x_ref[pl.ds(r * 128, 128), :].astype(F32)
             centred = xf - jnp.mean(xf, axis=-1, keepdims=True)
@@ -83,7 +89,7 @@
     @pl.when(step == steps - 1)
     def _():
         acc[...] = x_ref[...].astype(F32) + acc[...]
-        wdec = wdec_ref[...]
+        wdec = decoder[...]
         contract = (((1,), (1,)), ((), ()))
         for i in range(lon_all // SECTOR):
             main, halo = [], []
@@ -109,15 +115,19 @@
         grid=(hidden // FF_BLOCK,),
         in_specs=[
             pl.BlockSpec((tokens, width), lambda s: (0, 0)),
-            pl.BlockSpec((1, width), lambda s: (0, 0)),
+            pl.BlockSpec((width,), lambda s: (0,)),
             pl.BlockSpec((width, FF_BLOCK), lambda s: (0, s)),
             pl.BlockSpec((FF_BLOCK, width), lambda s: (s, 0)),
-            pl.BlockSpec((2 * HROWS, width), lambda s: (0, 0)),
+            pl.BlockSpec(w_dec.shape, lambda s: (0, 0)),
         ],
         out_specs=pl.BlockSpec((sectors, VROWS + HROWS, LANES), lambda s: (0, 0, 0)),
         out_shape=jax.ShapeDtypeStruct((sectors, VROWS + HROWS, LANES), BF16),
-        scratch_shapes=[pltpu.VMEM((tokens, width), BF16), pltpu.VMEM((tokens, width), F32)],
-        compiler_params=VMEM,
+        scratch_shapes=[
+            pltpu.VMEM((tokens, width), BF16),
+            pltpu.VMEM((tokens, width), F32),
+            pltpu.VMEM((2 * HROWS, width), BF16),
+        ],
+        compiler_params=LARGE,
         cost_estimate=pl.CostEstimate(
             flops=4 * tokens * width * hidden, bytes_accessed=4 * width * hidden, transcendentals=0
         ),
@@ -175,24 +185,26 @@
 
 def pairs_kernel(
     place_ref, recv_ref, obs_ref, err_ref, taper_ref, out_ref, anom_ref,
-    weighted, moved, weighted_halo, moved_halo, sums,
+    wide, weighted, moved, weighted_halo, moved_halo, sums,
 ):
     tiles = recv_ref.shape[0]
-    lon_all = obs_ref.shape[1]
-    obs = pltpu.roll(obs_ref[...], lax.rem(lon_all - SECTOR * place_ref[0], lon_all), 1)
-    first, last = obs[:, :LANES], obs[:, lon_all - LANES :]
-    lane = lanes_of(first.shape)
-    obs_main = copies_over_lanes(jnp.where(lane < SECTOR, first, 0.0), SECTOR)
-    obs_halo = jnp.where(
-        lane < HALO,
-        pltpu.roll(last, HALO, 1),
-        jnp.where(lane < 2 * HALO, pltpu.roll(first, LANES - SECTOR + HALO, 1), 0.0),
-    )
-    obs_halo = copies_over_lanes(obs_halo, 2 * HALO)
-    variables = VROWS - 3
-    err = err_ref[...]
-    prec_main = obs_main[variables : variables + 1] / (err * err)
-    prec_halo = obs_halo[variables : variables + 1] / (err * err)
+    lon_all, variables = obs_ref.shape
+    wide[...] = jnp.zeros_like(wide)
+    wide[0:lon_all, 0:variables] = obs_ref[...]
+    wide[lon_all : lon_all + 1, 0:variables] = err_ref[...].reshape(1, variables)
+    start = place_ref[0] * SECTOR
+
+    def columns(at, count):
+        return wide[pl.ds(pl.multiple_of(lax.rem(at + lon_all, lon_all), HALO), count), :]
+
+    around = [columns(start - HALO, HALO), columns(start + SECTOR, HALO)]
+    obs_main = jnp.concatenate([columns(start, SECTOR)] * GROUP, axis=0).T[:VROWS]
+    obs_halo = jnp.concatenate(around * (LANES // (2 * HALO)), axis=0).T[:VROWS]
+    err = jnp.broadcast_to(wide[lon_all : lon_all + 1, :], (LANES, LANES)).T[:VROWS]
+    is_variable = lax.broadcasted_iota(jnp.int32, err.shape, 0) < variables
+    each = jnp.where(is_variable, COUNT / (err * err), 0.0)
+    prec_main = jnp.where(obs_main < 0.5 * UNSEEN, each, 0.0)
+    prec_halo = jnp.where(obs_halo < 0.5 * UNSEEN, each, 0.0)
 
     sums[...] = jnp.zeros_like(sums)
 
@@ -256,13 +268,14 @@
             jax.ShapeDtypeStruct((tiles, VROWS, LANES), F32),
         ),
         scratch_shapes=[
+            pltpu.VMEM((obs.shape[0] + 8, LANES), F32),
             pltpu.VMEM((tiles, VROWS, LANES), F32),
             pltpu.VMEM((LANES // SECTOR, tiles, VROWS, LANES), F32),
             pltpu.VMEM((tiles // 2, VROWS, LANES), F32),
             pltpu.VMEM((LANES // (2 * HALO), tiles // 2, VROWS, LANES), F32),
             pltpu.VMEM((ROWS * tiles, 3 * LANES), F32),
         ],
-        compiler_params=VMEM,
+        compiler_params=SMALL,
         name="pairs",
     )(place, recv, obs, err, longitude_taper())
 
@@ -371,7 +384,7 @@
             pltpu.VMEM((GROUP, tiles, VROWS, LANES), F32),
             pltpu.VMEM((MEMBERS * tiles, LANES), F32),
         ],
-        compiler_params=VMEM,
+        compiler_params=SMALL,
         name="transform",
     )(lat_taper, recv, anomaly)
 
@@ -389,7 +402,7 @@
                 if j != m:
                     piece = pltpu.roll(piece, (SECTOR * (j - m)) % LANES, 1)
                 tile = piece if tile is None else jnp.where(group == j, piece, tile)
-            out_ref[m, :, pl.ds(c * LANES, LANES)] = tile[:variables]
+            out_ref[m, :, 0, pl.ds(c * LANES, LANES)] = tile[:variables]
 
 
 def strips(recv, variables):
@@ -399,8 +412,8 @@
         strips_kernel,
         in_specs=[full],
         out_specs=full,
-        out_shape=jax.ShapeDtypeStruct((GROUP, variables, tiles * SECTOR), F32),
-        compiler_params=VMEM,
+        out_shape=jax.ShapeDtypeStruct((GROUP, variables, 1, tiles * SECTOR), F32),
+        compiler_params=SMALL,
         name="strips",
     )(recv)
 
@@ -414,24 +427,22 @@
     ratio = lat_ids.astype(F32) / (RAD + 1.0)
     lat_taper = jnp.where(jnp.abs(lat_ids) <= RAD, (1.0 - ratio * ratio) ** 2, 0.0)
 
-    obs = jnp.concatenate([observed, obs_count[:1].astype(F32)], axis=0)
-    obs = lax.all_to_all(obs, "tile", split_axis=2, concat_axis=1, tiled=True)
-    obs = jnp.pad(obs.reshape(variables + 1, lon_all), ((0, VROWS - variables - 1), (0, 0)))
-    err = jnp.pad(obs_error, (0, VROWS - variables), constant_values=1.0).reshape(VROWS, 1)
+    seen = jnp.where(obs_count > 0, observed, UNSEEN)
+    obs = lax.all_to_all(jnp.transpose(seen, (2, 1, 0)), "tile", 0, 1, tiled=True)
 
     fields = forecast(
         hidden_in.reshape(mem_dev * tok_dev, width),
-        norm_gain.reshape(1, width),
+        norm_gain,
         w_in,
         w_out,
-        jnp.pad(w_dec, ((0, 2 * HROWS - variables), (0, 0))),
+        w_dec,
     )
     sectors = lax.all_to_all(fields, "mem", 0, 0, tiled=True)
-    smooth, anomaly = pairs(place, sectors, obs, err, lat_all)
+    smooth, anomaly = pairs(place, sectors, obs.reshape(lon_all, variables), obs_error, lat_all)
     rows = lax.all_to_all(smooth, "tile", 0, 0, tiled=True)
     increments = transform(lat_taper, rows, anomaly)
     back = lax.all_to_all(increments, "mem", 0, 0, tiled=True)
-    return strips(back, variables).reshape(mem_dev, variables, tok_dev // lon_all, lon_all)
+    return strips(back, variables)
 
 
 def solution(mesh):

time: 98.1 us -> 85.9 us (0.88)
  local copies, waits for them, and re-layouts: 8.72 us -> 0.01 us
  Pallas kernels: 36.7 us -> 33.7 us
  waiting for transfers between devices: 16.5 us -> 18.5 us
  blocking collectives: 9.51 us -> 7.91 us
    reshape x5 -> x0, local copies, waits for them, and re-layouts: 4.03 us -> none  [the longest x1 1.96 us: body(): strips(back, variables)]
    unnamed x7 -> x4, local copies, waits for them, and re-layouts: 2.46 us -> 0.01 us
    pad x2 -> x0, local copies, waits for them, and re-layouts: 2.24 us -> none  [the longest x1 1.58 us: body(): jnp.pad(w_dec, ((0, 2 * HROWS - variables), (0, 0)))]
    transpose x0 -> x1, other arithmetic: none -> 1.7 us  [body(): jnp.transpose(seen, (2, 1, 0))]
    all_to_all x1, blocking collectives: 9.51 us -> 7.91 us  [body(): back = lax.all_to_all(increments, 'mem', 0, 0, tiled=True)]
    all_to_all x1, waiting for transfers between devices: 5.41 us -> 6.89 us  [body(): sectors = lax.all_to_all(fields, 'mem', 0, 0, tiled=True)]
    pallas_call x1, Pallas kernels: 6.3 us -> 5.07 us  [transform(): pl.pallas_call(transform_kernel, in_specs=[pl.BlockSpec(memory_space=pltp...]
    pallas_call x1, Pallas kernels: 3.68 us -> 2.6 us  [pairs(): pl.pallas_call(pairs_kernel, in_specs=[pl.BlockSpec(memory_space=pltpu.SM...]
  transfers between devices with their start and end apart: 3 -> 3, of which waited for: 2 -> 2; matrix products, arithmetic and copies ran while one was open for 5% -> 0% of each run, Pallas kernels for 26% -> 30%
where the time goes in v1:
time: 85.9 us; the launch traced here: 84.3 us
  Pallas kernels  33.7 us (39%)
  starting transfers between devices  22.4 us (26%)
  waiting for transfers between devices  18.5 us (22%)
  blocking collectives  7.91 us (9%)
  other arithmetic  1.71 us (2%)
    pallas_call x1, Pallas kernels, forecast(): pl.pallas_call(forecast_kernel, grid=(hidden // FF_BLOCK,), in_specs=[pl....  25 us
    all_to_all x1, waiting for transfers between devices, body(): rows = lax.all_to_all(smooth, 'tile', 0, 0, tiled=True)  11.7 us
    all_to_all x1, starting transfers between devices, body(): lax.all_to_all(jnp.transpose(seen, (2, 1, 0)), 'tile', 0, 1, tiled=True)  9.13 us
    all_to_all x1, starting transfers between devices, body(): rows = lax.all_to_all(smooth, 'tile', 0, 0, tiled=True)  8.63 us
    all_to_all x1, blocking collectives, body(): back = lax.all_to_all(increments, 'mem', 0, 0, tiled=True)  7.91 us
    all_to_all x1, waiting for transfers between devices, body(): sectors = lax.all_to_all(fields, 'mem', 0, 0, tiled=True)  6.89 us
    pallas_call x1, Pallas kernels, transform(): pl.pallas_call(transform_kernel, in_specs=[pl.BlockSpec(memory_space=pltp...  5.07 us
    all_to_all x1, starting transfers between devices, body(): sectors = lax.all_to_all(fields, 'mem', 0, 0, tiled=True)  4.65 us
  transfers between devices with their start and end apart: 3, of which 2 were waited for; matrix products, arithmetic and copies ran while one was open for 0% of the time, Pallas kernels for 30%

profile of v1, /device:TPU:1, one launch (start us, length us, event | category | flops | bytes accessed | tf_op | source)
XLA Modules:
  0.0 84.3 jit_solution(14401962276106673408)
XLA Ops:
  0.0 1.7 %fusion = f32[16,16,69]{2,1,0:T(8,128)} fusion(f32[69,16,16]{0,2,1:T(8,128)} %param.14, s32[69,16,16]{0,2,1:T(8,128)} %param.15), kind=kLoop, calls=%fused_computation.1 | loop fusion | flops 35328 | bytes 211968 | tf_op jit(solution)/shard_map/transpose | solution.py:431
  1.7 9.1 %all-to-all-start.1 = ((f32[16,16,69]{2,1,0:T(8,128)}), f32[16,16,69]{2,1,0:T(8,128)S(1)}, u32[]{:S(2)}, u32[]{:S(2)}) async-start(f32[16,16,69]{2,1,0:T(8,128)} %fusion), calls=%async_computation.1 | async-start | bytes 262144 | tf_op jit(solution)/shard_map/all_to_all | solution.py:431
  10.8 0.0 copy-start
  10.8 0.0 copy-start.1
  10.9 25.0 %forecast.1 = bf16[8,112,128]{2,1,0:T(8,128)(2,1)} custom-call(bf16[1024,1024]{1,0:T(8,128)(2,1)} %bitcast.6, bf16[1024]{0:T(1024)(128)(2,1)} %gain_ref.1, bf16[1024,4096]{1,0:T(8,128)(2,1)} %win_ref.1, bf16[4096,1024]{1,0:T(8,128)(2,1)} %wout_ref.1, bf16[69,1024]{1,0:T(8,128)(2,1)} %wdec_ref.1), custom_call_target="tpu_custom_call" | custom-call | flops 17179869184 | bytes 16777216 | tf_op jit(solution)/shard_map/forecast/pallas_call | solution.py:113
  35.9 0.0 all-to-all-done.1
  35.9 4.6 %all-to-all-start = ((bf16[8,112,128]{2,1,0:T(8,128)(2,1)}), bf16[8,112,128]{2,1,0:T(8,128)(2,1)S(1)}, u32[]{:S(2)}, u32[]{:S(2)}) async-start(bf16[8,112,128]{2,1,0:T(8,128)(2,1)} %forecast.1), calls=%async_computation | async-start | bytes 458752 | tf_op jit(solution)/shard_map/all_to_all | solution.py:440
  40.5 6.9 %all-to-all-done.recv_ref = bf16[8,112,128]{2,1,0:T(8,128)(2,1)S(1)} async-done(((bf16[8,112,128]{2,1,0:T(8,128)(2,1)}), bf16[8,112,128]{2,1,0:T(8,128)(2,1)S(1)}, u32[]{:S(2)}, u32[]{:S(2)}) %all-to-all-start) | async-done | bytes 229408 | tf_op jit(solution)/shard_map/all_to_all | solution.py:440
  47.4 0.0 copy-done
  47.4 0.0 copy-done.1
  47.4 2.6 %pairs.1 = (bf16[16,144,128]{2,1,0:T(8,128)(2,1)}, f32[8,72,128]{2,1,0:T(8,128)S(1)}) custom-call(s32[1]{0:T(128)} %bitcast.place_ref, bf16[8,112,128]{2,1,0:T(8,128)(2,1)S(1)} %all-to-all-done.recv_ref, f32[256,69]{1,0:T(8,128)S(1)} %bitcast.5, f32[69]{0:T(128)S(1)} %copy-done.1, f32[384,128]{1,0:T(8,128)S(1)} %copy-done), custom_call_target="tpu_custom_call" | custom-call | tf_op jit(solution)/shard_map/pairs/pallas_call | solution.py:262
  50.0 8.6 %all-to-all-start.2 = ((bf16[16,144,128]{2,1,0:T(8,128)(2,1)}), bf16[16,144,128]{2,1,0:T(8,128)(2,1)S(1)}, u32[]{:S(2)}, u32[]{:S(2)}) async-start(bf16[16,144,128]{2,1,0:T(8,128)(2,1)} %get-tuple-element.7), calls=%async_computation.2 | async-start | bytes 1179648 | tf_op jit(solution)/shard_map/all_to_all | solution.py:442
  58.6 11.7 %all-to-all-done.2.recv_ref = bf16[16,144,128]{2,1,0:T(8,128)(2,1)S(1)} async-done(((bf16[16,144,128]{2,1,0:T(8,128)(2,1)}), bf16[16,144,128]{2,1,0:T(8,128)(2,1)S(1)}, u32[]{:S(2)}, u32[]{:S(2)}) %all-to-all-start.2) | async-done | bytes 589856 | tf_op jit(solution)/shard_map/all_to_all | solution.py:442
  70.3 5.1 %transform.1 = bf16[8,72,128]{2,1,0:T(8,128)(2,1)S(1)} custom-call(f32[16]{0:T(128)S(1)} %compare_select_fusion.lat_ref, bf16[16,144,128]{2,1,0:T(8,128)(2,1)S(1)} %all-to-all-done.2.recv_ref, f32[8,72,128]{2,1,0:T(8,128)S(1)} %get-tuple-element.8.anom_ref), custom_call_target="tpu_custom_call" | custom-call | tf_op jit(solution)/shard_map/transform/pallas_call | solution.py:377
  75.4 7.9 %all_to_all.24.recv_ref = bf16[8,72,128]{2,1,0:T(8,128)(2,1)S(1)} all-to-all(bf16[8,72,128]{2,1,0:T(8,128)(2,1)S(1)} %transform.1), channel_id=1, replica_groups=mesh['mem'=8,'tile'=16] {'mem'}, dimensions={0} | all-to-all | bytes 294912 | tf_op jit(solution)/shard_map/all_to_all | solution.py:444
  83.3 1.0 %strips.1 = f32[4,69,1,256]{3,2,1,0:T(1,128)} custom-call(bf16[8,72,128]{2,1,0:T(8,128)(2,1)S(1)} %all_to_all.24.recv_ref), custom_call_target="tpu_custom_call" | custom-call | tf_op jit(solution)/shard_map/strips/pallas_call | solution.py:411
  (1 shorter events, 0.0 us)
Async XLA Ops:
  1.7 34.2 %all-to-all-start.1 = ((f32[16,16,69]{2,1,0:T(8,128)}), f32[16,16,69]{2,1,0:T(8,128)S(1)}, u32[]{:S(2)}, u32[]{:S(2)}) async-start(f32[16,16,69]{2,1,0:T(8,128)} %fusion), calls=%async_computation.1 | async-start | bytes 262144 | tf_op jit(solution)/shard_map/all_to_all | solution.py:431
  10.8 36.6 %copy-start = (f32[384,128]{1,0:T(8,128)S(1)}, f32[384,128]{1,0:T(8,128)}, u32[]{:S(2)}) copy-start(f32[384,128]{1,0:T(8,128)} %constant.24.clone.taper_ref) | copy-start | bytes 589828
  10.8 36.6 %copy-start.1 = (f32[69]{0:T(128)S(1)}, f32[69]{0:T(128)}, u32[]{:S(2)}) copy-start(f32[69]{0:T(128)} %err_ref.1) | copy-start | bytes 832
  35.9 11.5 %all-to-all-start = ((bf16[8,112,128]{2,1,0:T(8,128)(2,1)}), bf16[8,112,128]{2,1,0:T(8,128)(2,1)S(1)}, u32[]{:S(2)}, u32[]{:S(2)}) async-start(bf16[8,112,128]{2,1,0:T(8,128)(2,1)} %forecast.1), calls=%async_computation | async-start | bytes 458752 | tf_op jit(solution)/shard_map/all_to_all | solution.py:440
  50.0 20.3 %all-to-all-start.2 = ((bf16[16,144,128]{2,1,0:T(8,128)(2,1)}), bf16[16,144,128]{2,1,0:T(8,128)(2,1)S(1)}, u32[]{:S(2)}, u32[]{:S(2)}) async-start(bf16[16,144,128]{2,1,0:T(8,128)(2,1)} %get-tuple-element.7), calls=%async_computation.2 | async-start | bytes 1179648 | tf_op jit(solution)/shard_map/all_to_all | solution.py:442

commit v2 on v1

v2 whole, which is shorter than its diff:
```python
import functools
import math

import jax
import jax.numpy as jnp
import numpy as np
from jax import lax
from jax.experimental import pallas as pl
from jax.experimental.pallas import tpu as pltpu
from jax.sharding import PartitionSpec as P

RAD = 6
NS_ITERS = 4
F32 = jnp.float32
BF16 = jnp.bfloat16

LANES = 128
VROWS = 72
HROWS = 40
CORES = 2
HALF = 16
HALO = 8
WINDOW = HALF + 2 * HALO
POINTS = CORES * HALF
MEMBERS = 32
GROUP = 4
DIAGS = MEMBERS // 2 + 1
ROWS = DIAGS + 1
FF_BLOCK = 1024
TOKEN_BLOCK = 512

UNSEEN = 1e30
COUNT = 3.0

LARGE = pltpu.CompilerParams(vmem_limit_bytes=60 * 2**20)
SMALL = pltpu.CompilerParams(vmem_limit_bytes=12 * 2**20)


def lanes_of(shape):
    return lax.broadcasted_iota(jnp.int32, shape, len(shape) - 1)


def gelu(h):
    inner = h * (math.sqrt(2.0 / math.pi) + (0.044715 * math.sqrt(2.0 / math.pi)) * (h * h))
    half = 0.5 * h
    return half + half * jnp.tanh(inner)


def forecast_kernel(x_ref, gain_ref, win_ref, wout_ref, wdec_ref, out_ref, normed, acc, decoder):
    step = pl.program_id(0)
    steps = pl.num_programs(0)
    tokens = x_ref.shape[0]
    blocks = tokens // TOKEN_BLOCK
    lon_all = tokens // GROUP

    @pl.when(step == 0)
    def _():
        gain = gain_ref[...].astype(F32).reshape(1, -1)
        decoder[...] = jnp.zeros_like(decoder)
        decoder[0 : wdec_ref.shape[0], :] = wdec_ref[...]
        for r in range(tokens // 128):
            xf = x_ref[pl.ds(r * 128, 128), :].astype(F32)
            centred = xf - jnp.mean(xf, axis=-1, keepdims=True)
            spread = jnp.mean(centred * centred, axis=-1, keepdims=True)
            normed[pl.ds(r * 128, 128), :] = (centred * lax.rsqrt(spread + 1e-05) * gain).astype(BF16)

    def up(r):
        return jnp.dot(
            normed[pl.ds(r * TOKEN_BLOCK, TOKEN_BLOCK), :], win_ref[...], preferred_element_type=F32
        )

    def run(first):
        hidden = up(0)
        for r in range(blocks):
            following = up(r + 1) if r + 1 < blocks else None
            down = jnp.dot(gelu(hidden).astype(BF16), wout_ref[...], preferred_element_type=F32)
            at = pl.ds(r * TOKEN_BLOCK, TOKEN_BLOCK)
            if first:
                acc[at, :] = down
            else:
                acc[at, :] += down
            hidden = following

    @pl.when(step == 0)
    def _():
        run(True)

    @pl.when(step > 0)
    def _():
        run(False)

    @pl.when(step == steps - 1)
    def _():
        acc[...] = x_ref[...].astype(F32) + acc[...]
        wdec = decoder[...]
        contract = (((1,), (1,)), ((), ()))
        for h in range(lon_all // HALF):
            window = []
            for m in range(GROUP):
                for at in (HALF * h, HALF * (h + 1)):
                    window.append(acc[pl.ds(m * lon_all + at % lon_all, HALF), :])
            window = jnp.concatenate(window, axis=0).astype(BF16)
            decoded = lax.dot_general(wdec, window, contract, preferred_element_type=F32)
            out_ref[h] = decoded[:VROWS].astype(BF16)


def forecast(x, gain, w_in, w_out, w_dec):
    tokens, width = x.shape
    hidden = w_in.shape[1]
    halves = tokens // GROUP // HALF
    return pl.pallas_call(
        forecast_kernel,
        grid=(hidden // FF_BLOCK,),
        in_specs=[
            pl.BlockSpec((tokens, width), lambda s: (0, 0)),
            pl.BlockSpec((width,), lambda s: (0,)),
            pl.BlockSpec((width, FF_BLOCK), lambda s: (0, s)),
            pl.BlockSpec((FF_BLOCK, width), lambda s: (s, 0)),
            pl.BlockSpec(w_dec.shape, lambda s: (0, 0)),
        ],
        out_specs=pl.BlockSpec((halves, VROWS, LANES), lambda s: (0, 0, 0)),
        out_shape=jax.ShapeDtypeStruct((halves, VROWS, LANES), BF16),
        scratch_shapes=[
            pltpu.VMEM((tokens, width), BF16),
            pltpu.VMEM((tokens, width), F32),
            pltpu.VMEM((2 * HROWS, width), BF16),
        ],
        compiler_params=LARGE,
        cost_estimate=pl.CostEstimate(
            flops=4 * tokens * width * hidden, bytes_accessed=4 * width * hidden, transcendentals=0
        ),
        name="forecast",
    )(x, gain, w_in, w_out, w_dec)


def sum_over_groups(tile, width):
    while width < LANES:
        tile = tile + pltpu.roll(tile, width, 1)
        width *= 2
    return tile


def shifted_tile(tiles, index, shift, width):
    move = shift * width
    if not move:
        return tiles(index)
    here = pltpu.roll(tiles(index), LANES - move, 1)
    there = pltpu.roll(tiles(index + 1), LANES - move, 1)
    return jnp.where(lanes_of(here.shape) < LANES - move, here, there)


def pair_sums(fields, observed, prec, width, weighted, moved, put):
    count = len(fields)
    per = LANES // width
    total = fields[0]
    for tile in fields[1:]:
        total = total + tile
    mean = sum_over_groups(total, width) / MEMBERS
    anomalies = []
    for k in range(count):
        anomaly = fields[k] - mean
        anomalies.append(anomaly)
        weighted[k] = (anomaly * prec).astype(BF16).astype(F32)
        moved[0, k] = anomaly.astype(BF16).astype(F32)
    for t in range(1, per):
        for k in range(count):
            moved[t, k] = shifted_tile(lambda j: moved[0, j % count], k, t, width)
    innovation = observed - mean
    for k in range(count):
        put(DIAGS, k, jnp.sum(weighted[k] * innovation, axis=0, keepdims=True))
    for s in range(DIAGS):
        on, t = divmod(s, per)
        for k in range(count):
            put(s, k, jnp.sum(weighted[k] * moved[t, (k + on) % count], axis=0, keepdims=True))
    return anomalies


def pairs_kernel(
    recv_ref, west_ref, east_ref, err_ref, taper_ref, out_ref, anom_ref,
    wide, weighted, moved, sums,
):
    tiles = recv_ref.shape[0] // CORES
    variables = west_ref.shape[2]
    wide[...] = jnp.zeros_like(wide)
    wide[0:1, 0:variables] = err_ref[...].reshape(1, variables)
    err = jnp.broadcast_to(wide[0:1, :], (LANES, LANES)).T[:VROWS]
    is_variable = lax.broadcasted_iota(jnp.int32, err.shape, 0) < variables
    each = jnp.where(is_variable, COUNT / (err * err), 0.0)

    anomalies = []
    for r in range(CORES):
        wide[0:HALF, 0:variables] = west_ref[r]
        wide[HALF:WINDOW, 0:variables] = east_ref[r]
        obs = jnp.concatenate([wide[...]] * GROUP, axis=0).T[:VROWS]
        prec = jnp.where(obs < 0.5 * UNSEEN, each, 0.0)

        def put(s, k, row):
            sums[pl.ds(s * tiles + k, 1), r * LANES : (r + 1) * LANES] = row

        fields = [recv_ref[CORES * m + r].astype(F32) for m in range(tiles)]
        anomalies.append(
            pair_sums(fields, obs, prec, WINDOW, weighted.at[r], moved.at[r], put)
        )
    lower = lanes_of((VROWS, LANES)) % POINTS < HALF
    for k in range(tiles):
        anom_ref[k] = jnp.where(
            lower,
            pltpu.roll(anomalies[0][k], LANES - HALO, 1),
            pltpu.roll(anomalies[1][k], HALF - HALO, 1),
        )
    smooth = jnp.dot(
        sums[...], taper_ref[...], precision=lax.Precision.HIGHEST, preferred_element_type=F32
    ).astype(BF16)
    for c in range(out_ref.shape[0]):
        out_ref[c] = smooth


def taper_of(offset):
    offset = np.asarray(offset, np.float32)
    ratio = offset / np.float32(RAD + 1.0)
    return np.where(np.abs(offset) <= RAD, (1.0 - ratio * ratio) ** 2, 0.0).astype(np.float32)


def longitude_taper():
    lat, rest = np.divmod(np.arange(CORES * LANES), LANES)
    member, col = np.divmod(rest, WINDOW)
    out_member, rest = np.divmod(np.arange(LANES), POINTS)
    out_lat, out_col = np.divmod(rest, HALF)
    same = (lat[:, None] == out_lat[None, :]) & (member[:, None] == out_member[None, :])
    weight = taper_of(col[:, None] - HALO - out_col[None, :])
    return jnp.asarray(np.where(same, weight, 0.0).astype(np.float32))


def pairs(recv, obs, err, chips):
    tiles = recv.shape[0] // CORES
    full = pl.BlockSpec(memory_space=pltpu.VMEM)
    return pl.pallas_call(
        pairs_kernel,
        in_specs=[full] * 5,
        out_specs=(full, full),
        out_shape=(
            jax.ShapeDtypeStruct((chips, ROWS * tiles, LANES), BF16),
            jax.ShapeDtypeStruct((tiles, VROWS, LANES), F32),
        ),
        scratch_shapes=[
            pltpu.VMEM((WINDOW, LANES), F32),
            pltpu.VMEM((CORES, tiles, VROWS, LANES), F32),
            pltpu.VMEM((CORES, LANES // WINDOW, tiles, VROWS, LANES), F32),
            pltpu.VMEM((ROWS * tiles, CORES * LANES), F32),
        ],
        compiler_params=SMALL,
        name="pairs",
    )(recv, *obs, err, longitude_taper())


def on_by(x, n):
    sub, t = divmod(n % MEMBERS, GROUP)
    if t:
        move = LANES - POINTS * t
        x = pltpu.roll(x, move, 1)
        x = jnp.where(lanes_of(x.shape) < move, x, pltpu.roll(x, 7, 0))
    if sub:
        x = pltpu.roll(x, 8 - sub, 0)
    return x


def shifted_sum(term):
    total = None
    for t in range(GROUP - 1, -1, -1):
        inner = None
        for a in range(MEMBERS // GROUP - 1, -1, -1):
            part = term(GROUP * a + t)
            inner = part if inner is None else on_by(inner, GROUP) + part
        total = inner if total is None else on_by(total, 1) + inner
    return total


def product(left, right, out, scale=None, shift=None):
    for s in range(DIAGS):
        value = shifted_sum(lambda t: left[(-t) % MEMBERS] * right[(s - t) % MEMBERS])
        if scale is not None:
            value = scale * value
            if s == 0:
                value = value + shift
        out[s] = value
    mirror(out)


def mirror(out):
    for s in range(1, MEMBERS - DIAGS + 1):
        out[MEMBERS - s] = on_by(out[s], -s)


def latitude_weight(offset):
    ratio = offset.astype(F32) * (1.0 / (RAD + 1.0))
    return jnp.where(jnp.abs(offset) <= RAD, (1.0 - ratio * ratio) * (1.0 - ratio * ratio), 0.0)


def transform_kernel(place_ref, recv_ref, anom_ref, out_ref, bank, moved, coeff):
    chips = recv_ref.shape[0]
    tiles = anom_ref.shape[0]
    same, south, north = None, None, None
    for c in range(chips):
        sums = recv_ref[c].astype(F32)
        offset = CORES * (place_ref[0] - c)
        parts = [latitude_weight(offset + d) * sums for d in (0, -1, 1)]
        if c == 0:
            same, south, north = parts
        else:
            same, south, north = same + parts[0], south + parts[1], north + parts[2]
    lower = lanes_of(same.shape) % POINTS < HALF
    local = same + jnp.where(
        lower, pltpu.roll(south, LANES - HALF, 1), pltpu.roll(north, HALF, 1)
    )
    diag = [local[s * tiles : (s + 1) * tiles] for s in range(ROWS)]
    innov = diag[DIAGS]
    diag[0] = diag[0] + (MEMBERS - 1.0)
    gram, root, inv_root, corr = bank.at[0], bank.at[1], bank.at[2], bank.at[3]
    other_root, other_inv = bank.at[4], bank.at[5]
    square = None
    for s in range(DIAGS):
        part = diag[s] * diag[s]
        if 0 < s < DIAGS - 1:
            part = part + part
        square = part if square is None else square + part
    square = jnp.broadcast_to(jnp.sum(square, axis=0, keepdims=True), square.shape)
    frob = jnp.sqrt(sum_over_groups(square, POINTS))
    inv_frob = 1.0 / frob
    for s in range(DIAGS):
        gram[s] = diag[s] * inv_frob
    mirror(gram)
    for s in range(MEMBERS):
        inv_root[s] = -0.5 * gram[s] + (1.5 if s == 0 else 0.0)
    product(gram, inv_root, root)
    for sweep in range(1, NS_ITERS):
        product(inv_root, root, corr, -0.5, 1.5)
        if sweep < NS_ITERS - 1:
            product(root, corr, other_root)
        product(corr, inv_root, other_inv)
        root, other_root = other_root, root
        inv_root, other_inv = other_inv, inv_root
    half = shifted_sum(lambda t: inv_root[(-t) % MEMBERS] * innov)
    mean_weights = shifted_sum(lambda t: inv_root[(-t) % MEMBERS] * half) * inv_frob
    factor = math.sqrt(MEMBERS - 1.0) / jnp.sqrt(frob)
    for s in range(MEMBERS):
        value = inv_root[s] * factor + on_by(mean_weights, s)
        coeff[pl.ds(s * tiles, tiles), :] = value.astype(BF16).astype(F32)
    for k in range(tiles):
        moved[0, k] = anom_ref[k].astype(BF16).astype(F32)
    for t in range(1, GROUP):
        for k in range(tiles):
            moved[t, k] = shifted_tile(lambda j: moved[0, j % tiles], k, t, POINTS)
    for k in range(tiles):
        mixed = None
        for s in range(MEMBERS):
            on, t = divmod(s, GROUP)
            part = moved[t, (k + on) % tiles] * coeff[pl.ds(s * tiles + k, 1), :]
            mixed = part if mixed is None else mixed + part
        mixed = mixed - anom_ref[k]
        low = mixed[:HROWS]
        high = jnp.concatenate([mixed[HROWS:], jnp.zeros((2 * HROWS - VROWS, LANES), F32)], axis=0)
        first = lanes_of(low.shape) % POINTS < HALF
        out_ref[CORES * k] = jnp.where(first, low, pltpu.roll(high, HALF, 1)).astype(BF16)
        out_ref[CORES * k + 1] = jnp.where(first, pltpu.roll(low, LANES - HALF, 1), high).astype(BF16)


def transform(place, recv, anomaly):
    tiles = anomaly.shape[0]
    full = pl.BlockSpec(memory_space=pltpu.VMEM)
    return pl.pallas_call(
        transform_kernel,
        in_specs=[pl.BlockSpec(memory_space=pltpu.SMEM), full, full],
        out_specs=full,
        out_shape=jax.ShapeDtypeStruct((CORES * tiles, HROWS, LANES), BF16),
        scratch_shapes=[
            pltpu.VMEM((6, MEMBERS, tiles, LANES), F32),
            pltpu.VMEM((GROUP, tiles, VROWS, LANES), F32),
            pltpu.VMEM((MEMBERS * tiles, LANES), F32),
        ],
        compiler_params=SMALL,
        name="transform",
    )(place, recv, anomaly)


def strips_kernel(recv_ref, out_ref):
    halves = recv_ref.shape[0]
    variables = out_ref.shape[1]
    per = LANES // HALF
    parts = [recv_ref[h].astype(F32) for h in range(halves)]
    group = lax.rem(lanes_of(parts[0].shape) + (LANES - HALO), LANES) // HALF
    first = lanes_of(parts[0].shape) < HALO
    for m in range(GROUP):
        for side in range(2):
            tiles = []
            for c in range(halves // per):
                tile = None
                for j in range(per):
                    piece = parts[per * c + j]
                    move = (HALF * (j - side) - POINTS * m + HALO) % LANES
                    if move:
                        piece = pltpu.roll(piece, move, 1)
                    tile = piece if tile is None else jnp.where(group == j, piece, tile)
                tiles.append(tile)
            for c in range(len(tiles)):
                tile = jnp.where(first, tiles[c - 1], tiles[c])
                at = pl.ds(c * LANES, LANES)
                if side == 0:
                    out_ref[m, 0:HROWS, 0, at] = tile
                else:
                    out_ref[m, HROWS:variables, 0, at] = tile[: variables - HROWS]


def strips(recv, variables):
    halves = recv.shape[0]
    full = pl.BlockSpec(memory_space=pltpu.VMEM)
    return pl.pallas_call(
        strips_kernel,
        in_specs=[full],
        out_specs=full,
        out_shape=jax.ShapeDtypeStruct((GROUP, variables, 1, halves * HALF), F32),
        compiler_params=SMALL,
        name="strips",
    )(recv)


def body(hidden_in, norm_gain, w_in, w_out, w_dec, observed, obs_count, obs_error):
    mem_dev, tok_dev, width = hidden_in.shape
    variables, lon_dev, lat_all = observed.shape
    n_mem, n_tile = lax.axis_size("mem"), lax.axis_size("tile")
    chips = n_tile // CORES
    mem, tile = lax.axis_index("mem"), lax.axis_index("tile")
    place = lax.div(tile, CORES).astype(jnp.int32).reshape(1)
    by_chip = [
        [m * n_tile + c * CORES + k for m in range(n_mem) for k in range(CORES)] for c in range(chips)
    ]
    by_core = [[c * CORES + k for c in range(chips)] for k in range(CORES)]

    seen = jnp.where(obs_count > 0, observed, UNSEEN)
    seen = lax.dynamic_slice_in_dim(seen, CORES * mem, CORES, 2)
    seen = jnp.transpose(seen, (2, 1, 0))

    def to_sector(part, move):
        pairs_of = []
        for m in range(n_mem):
            for j in range(n_tile):
                to = (j + move) % n_tile
                pairs_of.append((m * n_tile + j, to // CORES * n_tile + CORES * m + to % CORES))
        return lax.ppermute(part, ("mem", "tile"), pairs_of)

    obs = [to_sector(seen, 0), to_sector(seen, -1)]

    fields = forecast(
        hidden_in.reshape(mem_dev * tok_dev, width), norm_gain, w_in, w_out, w_dec
    )
    halves = lax.all_to_all(
        fields, ("mem", "tile"), 0, 0, tiled=True, axis_index_groups=by_chip
    )
    smooth, anomaly = pairs(halves, obs, obs_error, chips)
    rows = lax.all_to_all(smooth, "tile", 0, 0, tiled=True, axis_index_groups=by_core)
    increments = transform(place, rows, anomaly)
    back = lax.all_to_all(
        increments, ("mem", "tile"), 0, 0, tiled=True, axis_index_groups=by_chip
    )
    return strips(back, variables)


def solution(mesh):
    return jax.shard_map(
        body,
        mesh=mesh,
        in_specs=(
            P("mem", "tile", None),
            P(),
            P(),
            P(),
            P(),
            P(None, "tile", None),
            P(None, "tile", None),
            P(),
        ),
        out_specs=P("mem", None, "tile", None),
        check_vma=False,
    )
```

time: 85.9 us -> 81.3 us (0.946); the launches traced: 84.3 us -> 80.9 us
  waiting for transfers between devices: 18.5 us -> 12.9 us
  blocking collectives: 7.91 us -> 13.1 us
  starting transfers between devices: 22.4 us -> 19.9 us
  other arithmetic: 1.71 us -> 0.01 us
  local copies, waits for them, and re-layouts: 0.01 us -> 0.88 us
    all_to_all x3 -> x2, waiting for transfers between devices: 18.5 us -> 8.82 us  [the longest x1 7.42 us: body(): lax.all_to_all(smooth, 'tile', 0, 0, tiled=True, axis_index_groups=by_core)]
    all_to_all x1, blocking collectives: 7.91 us -> 13.1 us  [body(): lax.all_to_all(increments, ('mem', 'tile'), 0, 0, tiled=True, axis_index_...]
    ppermute x0 -> x2, waiting for transfers between devices: none -> 4.08 us  [to_sector(): return lax.ppermute(part, ('mem', 'tile'), pairs_of)]
    all_to_all x3 -> x2, starting transfers between devices: 22.4 us -> 18.9 us  [the longest x1 11.5 us: body(): lax.all_to_all(smooth, 'tile', 0, 0, tiled=True, axis_index_groups=by_core)]
    transpose x1, other arithmetic: 1.7 us -> 0.01 us  [body(): seen = jnp.transpose(seen, (2, 1, 0))]
    ppermute x0 -> x2, starting transfers between devices: none -> 1.01 us  [to_sector(): return lax.ppermute(part, ('mem', 'tile'), pairs_of)]
    dynamic_slice x0 -> x2, local copies, waits for them, and re-layouts: none -> 0.87 us  [body(): seen = lax.dynamic_slice_in_dim(seen, CORES * mem, CORES, 2)]
  transfers between devices with their start and end apart: 3 -> 4, of which waited for: 2 -> 3; matrix products, arithmetic and copies ran while one was open for 0% -> 1% of each run, Pallas kernels for 30% -> 0%
where the time goes in v2:
time: 81.3 us; the launch traced here: 80.9 us
  Pallas kernels  34.1 us (42%)
  starting transfers between devices  19.9 us (24%)
  blocking collectives  13.1 us (16%)
  waiting for transfers between devices  12.9 us (16%)
  local copies, waits for them, and re-layouts  0.88 us (1%)
    pallas_call x1, Pallas kernels, forecast(): pl.pallas_call(forecast_kernel, grid=(hidden // FF_BLOCK,), in_specs=[pl....  25.4 us
    all_to_all x1, blocking collectives, body(): lax.all_to_all(increments, ('mem', 'tile'), 0, 0, tiled=True, axis_index_...  13.1 us
    all_to_all x1, starting transfers between devices, body(): lax.all_to_all(smooth, 'tile', 0, 0, tiled=True, axis_index_groups=by_core)  11.5 us
    all_to_all x1, waiting for transfers between devices, body(): lax.all_to_all(smooth, 'tile', 0, 0, tiled=True, axis_index_groups=by_core)  7.42 us
    all_to_all x1, starting transfers between devices, body(): lax.all_to_all(fields, ('mem', 'tile'), 0, 0, tiled=True, axis_index_grou...  7.33 us
    pallas_call x1, Pallas kernels, transform(): pl.pallas_call(transform_kernel, in_specs=[pl.BlockSpec(memory_space=pltp...  4.94 us
    ppermute x2, waiting for transfers between devices, to_sector(): return lax.ppermute(part, ('mem', 'tile'), pairs_of)  4.08 us
    pallas_call x1, Pallas kernels, pairs(): pl.pallas_call(pairs_kernel, in_specs=[full] * 5, out_specs=(full, full),...  2.62 us
  transfers between devices with their start and end apart: 4, of which 3 were waited for; matrix products, arithmetic and copies ran while one was open for 1% of the time, Pallas kernels for 0%

profile of v2, /device:TPU:1, one launch (start us, length us, event | category | flops | bytes accessed | tf_op | source)
XLA Modules:
  0.0 80.9 jit_solution(10505030845067358236)
XLA Ops:
  0.0 0.0 copy-start
  0.0 0.0 copy-start.1
  0.0 0.0 copy-start.2
  0.0 25.4 %forecast.1 = bf16[16,72,128]{2,1,0:T(8,128)(2,1)} custom-call(bf16[1024,1024]{1,0:T(8,128)(2,1)} %bitcast.4, bf16[1024]{0:T(1024)(128)(2,1)} %gain_ref.1, bf16[1024,4096]{1,0:T(8,128)(2,1)} %win_ref.1, bf16[4096,1024]{1,0:T(8,128)(2,1)} %wout_ref.1, bf16[69,1024]{1,0:T(8,128)(2,1)} %wdec_ref.1), custom_call_target="tpu_custom_call" | custom-call | flops 17179869184 | bytes 16777216 | tf_op jit(solution)/shard_map/forecast/pallas_call | solution.py:111
  25.4 7.3 %all-to-all-start = ((bf16[16,72,128]{2,1,0:T(8,128)(2,1)}), bf16[16,72,128]{2,1,0:T(8,128)(2,1)S(1)}, u32[]{:S(2)}, u32[]{:S(2)}) async-start(bf16[16,72,128]{2,1,0:T(8,128)(2,1)} %forecast.1), calls=%async_computation | async-start | bytes 589824 | tf_op jit(solution)/shard_map/all_to_all | solution.py:455
  32.8 0.0 copy-done
  32.8 0.9 %constant_dynamic-slice_fusion = s32[69,16,2]{0,2,1:T(2,128)S(1)} fusion(s32[69,16,16]{0,2,1:T(8,128)} %param.15, s32[]{:T(128)S(6)} %select_n.8), kind=kLoop, calls=%fused_computation.3 | loop fusion | bytes 17668 | tf_op jit(solution)/shard_map/dynamic_slice | solution.py:439
  33.6 0.2 collective-permute-start.1
  33.8 0.8 %collective-permute-start = (f32[2,16,69]{2,1,0:T(8,128)S(1)}, f32[2,16,69]{2,1,0:T(8,128)S(1)}, u32[]{:S(2)}, u32[]{:S(2)}) collective-permute-start(f32[2,16,69]{2,1,0:T(8,128)S(1)} %fusion), channel_id=1, source_target_pairs={{0,0},{1,1},{2,16},{3,17},{4,32},{5,33},{6,48},{7,49},{8,64},{9,65... | collective-permute-start | bytes 26504 | tf_op jit(solution)/shard_map/ppermute | solution.py:448
  34.7 4.1 %collective-permute-done.1.east_ref = f32[2,16,69]{2,1,0:T(8,128)S(1)} collective-permute-done((f32[2,16,69]{2,1,0:T(8,128)S(1)}, f32[2,16,69]{2,1,0:T(8,128)S(1)}, u32[]{:S(2)}, u32[]{:S(2)}) %collective-permute-start.1) | collective-permute-done | bytes 8864 | tf_op jit(solution)/shard_map/ppermute | solution.py:448
  38.7 0.0 collective-permute-done.west_ref
  38.8 1.4 %all-to-all-done.recv_ref = bf16[16,72,128]{2,1,0:T(8,128)(2,1)S(1)} async-done(((bf16[16,72,128]{2,1,0:T(8,128)(2,1)}), bf16[16,72,128]{2,1,0:T(8,128)(2,1)S(1)}, u32[]{:S(2)}, u32[]{:S(2)}) %all-to-all-start) | async-done | bytes 294944 | tf_op jit(solution)/shard_map/all_to_all | solution.py:455
  40.2 0.0 copy-done.1
  40.2 0.0 copy-done.2
  40.2 2.6 %pairs.1 = (bf16[8,144,128]{2,1,0:T(8,128)(2,1)}, f32[8,72,128]{2,1,0:T(8,128)S(1)}) custom-call(bf16[16,72,128]{2,1,0:T(8,128)(2,1)S(1)} %all-to-all-done.recv_ref, f32[2,16,69]{2,1,0:T(8,128)S(1)} %collective-permute-done.west_ref, f32[2,16,69]{2,1,0:T(8,128)S(1)} %collective-permute-done.1.east_ref, f32[69]{0:T(128)S(1)} %copy-done.2, ...), custom_call_target="tpu_custom_call" | custom-call | tf_op jit(solution)/shard_map/pairs/pallas_call | solution.py:237
  42.8 11.5 %all-to-all-start.1 = ((bf16[8,144,128]{2,1,0:T(8,128)(2,1)}), bf16[8,144,128]{2,1,0:T(8,128)(2,1)S(1)}, u32[]{:S(2)}, u32[]{:S(2)}) async-start(bf16[8,144,128]{2,1,0:T(8,128)(2,1)} %get-tuple-element.7), calls=%async_computation.1 | async-start | bytes 589824 | tf_op jit(solution)/shard_map/all_to_all | solution.py:459
  54.3 7.4 %all-to-all-done.1.recv_ref = bf16[8,144,128]{2,1,0:T(8,128)(2,1)S(1)} async-done(((bf16[8,144,128]{2,1,0:T(8,128)(2,1)}), bf16[8,144,128]{2,1,0:T(8,128)(2,1)S(1)}, u32[]{:S(2)}, u32[]{:S(2)}) %all-to-all-start.1) | async-done | bytes 294944 | tf_op jit(solution)/shard_map/all_to_all | solution.py:459
  61.7 4.9 %transform.1 = bf16[16,40,128]{2,1,0:T(8,128)(2,1)S(1)} custom-call(s32[1]{0:T(128)} %bitcast.place_ref, bf16[8,144,128]{2,1,0:T(8,128)(2,1)S(1)} %all-to-all-done.1.recv_ref, f32[8,72,128]{2,1,0:T(8,128)S(1)} %get-tuple-element.8.anom_ref), custom_call_target="tpu_custom_call" | custom-call | tf_op jit(solution)/shard_map/transform/pallas_call | solution.py:370
  66.7 13.1 %all_to_all.15.recv_ref = bf16[16,40,128]{2,1,0:T(8,128)(2,1)S(1)} all-to-all(bf16[16,40,128]{2,1,0:T(8,128)(2,1)S(1)} %transform.1), channel_id=1, replica_groups={{0,1,16,17,32,33,48,49,64,65,80,81,96,97,112,113},{2,3,18,19,34,35,50,5..., dimensions={0} | all-to-all | bytes 327680 | tf_op jit(solution)/shard_map/all_to_all | solution.py:461
  79.8 1.1 %strips.1 = f32[4,69,1,256]{3,2,1,0:T(1,128)} custom-call(bf16[16,40,128]{2,1,0:T(8,128)(2,1)S(1)} %all_to_all.15.recv_ref), custom_call_target="tpu_custom_call" | custom-call | tf_op jit(solution)/shard_map/strips/pallas_call | solution.py:416
  (2 shorter events, 0.0 us)
Async XLA Ops:
  0.0 32.8 %copy-start = (f32[69,16,16]{0,2,1:T(8,128)S(1)}, f32[69,16,16]{0,2,1:T(8,128)}, u32[]{:S(2)}) copy-start(f32[69,16,16]{0,2,1:T(8,128)} %param.14) | copy-start | bytes 211972
  0.0 40.2 %copy-start.1 = (f32[256,128]{1,0:T(8,128)S(1)}, f32[256,128]{1,0:T(8,128)}, u32[]{:S(2)}) copy-start(f32[256,128]{1,0:T(8,128)} %constant.23.clone.taper_ref) | copy-start | bytes 393220
  0.0 40.2 %copy-start.2 = (f32[69]{0:T(128)S(1)}, f32[69]{0:T(128)}, u32[]{:S(2)}) copy-start(f32[69]{0:T(128)} %err_ref.1) | copy-start | bytes 832
  25.4 14.7 %all-to-all-start = ((bf16[16,72,128]{2,1,0:T(8,128)(2,1)}), bf16[16,72,128]{2,1,0:T(8,128)(2,1)S(1)}, u32[]{:S(2)}, u32[]{:S(2)}) async-start(bf16[16,72,128]{2,1,0:T(8,128)(2,1)} %forecast.1), calls=%async_computation | async-start | bytes 589824 | tf_op jit(solution)/shard_map/all_to_all | solution.py:455
  33.6 5.1 %collective-permute-start.1 = (f32[2,16,69]{2,1,0:T(8,128)S(1)}, f32[2,16,69]{2,1,0:T(8,128)S(1)}, u32[]{:S(2)}, u32[]{:S(2)}) collective-permute-start(f32[2,16,69]{2,1,0:T(8,128)S(1)} %fusion), channel_id=1, source_target_pairs={{0,113},{1,0},{2,1},{3,16},{4,17},{5,32},{6,33},{7,48},{8,49},{9,6... | collective-permute-start | bytes 26504 | tf_op jit(solution)/shard_map/ppermute | solution.py:448
  33.8 4.9 %collective-permute-start = (f32[2,16,69]{2,1,0:T(8,128)S(1)}, f32[2,16,69]{2,1,0:T(8,128)S(1)}, u32[]{:S(2)}, u32[]{:S(2)}) collective-permute-start(f32[2,16,69]{2,1,0:T(8,128)S(1)} %fusion), channel_id=1, source_target_pairs={{0,0},{1,1},{2,16},{3,17},{4,32},{5,33},{6,48},{7,49},{8,64},{9,65... | collective-permute-start | bytes 26504 | tf_op jit(solution)/shard_map/ppermute | solution.py:448
  42.8 18.9 %all-to-all-start.1 = ((bf16[8,144,128]{2,1,0:T(8,128)(2,1)}), bf16[8,144,128]{2,1,0:T(8,128)(2,1)S(1)}, u32[]{:S(2)}, u32[]{:S(2)}) async-start(bf16[8,144,128]{2,1,0:T(8,128)(2,1)} %get-tuple-element.7), calls=%async_computation.1 | async-start | bytes 589824 | tf_op jit(solution)/shard_map/all_to_all | solution.py:459

commit v3 on v2

--- a/solution.py
+++ b/solution.py
@@ -46,7 +46,41 @@
     return half + half * jnp.tanh(inner)
 
 
-def forecast_kernel(x_ref, gain_ref, win_ref, wout_ref, wdec_ref, out_ref, normed, acc, decoder):
+SENDS = (0, -1)
+
+
+def served(mem, tile, move, ways):
+    n_tile, n_y = ways
+    half = lax.rem(tile + (n_tile + move), n_tile)
+    to_mem = lax.div(half, CORES)
+    z_lo, y = lax.div(mem, n_y), lax.rem(mem, n_y)
+    to_z_lo, to_y = lax.div(to_mem, n_y), lax.rem(to_mem, n_y)
+    chip = lax.div(tile, CORES)
+    x, z_hi = lax.div(chip, 2), lax.rem(chip, 2)
+    n_x = n_tile // (2 * CORES)
+    to_x = lax.rem(x + 2 + to_y - y + 2 * n_x, n_x)
+    to_z_hi = lax.rem(z_hi + z_lo + to_z_lo, 2)
+    return half, 2 * to_x + to_z_hi
+
+
+def served_here(mem, tile, move, ways):
+    n_tile, n_y = ways
+    half = (tile + n_tile + move) % n_tile
+    to_mem = half // CORES
+    z_lo, y = mem // n_y, mem % n_y
+    to_z_lo, to_y = to_mem // n_y, to_mem % n_y
+    chip = tile // CORES
+    x, z_hi = chip // 2, chip % 2
+    n_x = n_tile // (2 * CORES)
+    to_x = (x + 2 + to_y - y) % n_x
+    to_z_hi = (z_hi + z_lo + to_z_lo) % 2
+    return half, 2 * to_x + to_z_hi
+
+
+def forecast_kernel(
+    place_ref, x_ref, gain_ref, win_ref, wout_ref, wdec_ref, obs_ref, count_ref, out_ref, west_ref, east_ref,
+    normed, acc, decoder, *, n_y,
+):
     step = pl.program_id(0)
     steps = pl.num_programs(0)
     tokens = x_ref.shape[0]
@@ -56,6 +90,13 @@
     @pl.when(step == 0)
     def _():
         gain = gain_ref[...].astype(F32).reshape(1, -1)
+        n_tile = out_ref.shape[0]
+        mem, tile = lax.div(place_ref[0], n_tile), lax.rem(place_ref[0], n_tile)
+        for seen_ref, move in zip((west_ref, east_ref), SENDS):
+            _, chip = served(mem, tile, move, (n_tile, n_y))
+            for r in range(CORES):
+                row = CORES * chip + r
+                seen_ref[r] = jnp.where(count_ref[:, row, :] > 0, obs_ref[:, row, :], UNSEEN)
         decoder[...] = jnp.zeros_like(decoder)
         decoder[0 : wdec_ref.shape[0], :] = wdec_ref[...]
         for r in range(tokens // 128):
@@ -104,22 +145,35 @@
             out_ref[h] = decoded[:VROWS].astype(BF16)
 
 
-def forecast(x, gain, w_in, w_out, w_dec):
+def forecast(place, n_y, x, gain, w_in, w_out, w_dec, observed, obs_count):
     tokens, width = x.shape
     hidden = w_in.shape[1]
     halves = tokens // GROUP // HALF
+    lon_dev, _, variables = observed.shape
+    whole = pl.BlockSpec(observed.shape, lambda s: (0, 0, 0))
     return pl.pallas_call(
-        forecast_kernel,
+        functools.partial(forecast_kernel, n_y=n_y),
         grid=(hidden // FF_BLOCK,),
         in_specs=[
+            pl.BlockSpec(memory_space=pltpu.SMEM),
             pl.BlockSpec((tokens, width), lambda s: (0, 0)),
             pl.BlockSpec((width,), lambda s: (0,)),
             pl.BlockSpec((width, FF_BLOCK), lambda s: (0, s)),
             pl.BlockSpec((FF_BLOCK, width), lambda s: (s, 0)),
             pl.BlockSpec(w_dec.shape, lambda s: (0, 0)),
+            whole,
+            whole,
         ],
-        out_specs=pl.BlockSpec((halves, VROWS, LANES), lambda s: (0, 0, 0)),
-        out_shape=jax.ShapeDtypeStruct((halves, VROWS, LANES), BF16),
+        out_specs=(
+            pl.BlockSpec((halves, VROWS, LANES), lambda s: (0, 0, 0)),
+            pl.BlockSpec((CORES, lon_dev, variables), lambda s: (0, 0, 0)),
+            pl.BlockSpec((CORES, lon_dev, variables), lambda s: (0, 0, 0)),
+        ),
+        out_shape=(
+            jax.ShapeDtypeStruct((halves, VROWS, LANES), BF16),
+            jax.ShapeDtypeStruct((CORES, lon_dev, variables), F32),
+            jax.ShapeDtypeStruct((CORES, lon_dev, variables), F32),
+        ),
         scratch_shapes=[
             pltpu.VMEM((tokens, width), BF16),
             pltpu.VMEM((tokens, width), F32),
@@ -130,7 +184,7 @@
             flops=4 * tokens * width * hidden, bytes_accessed=4 * width * hidden, transcendentals=0
         ),
         name="forecast",
-    )(x, gain, w_in, w_out, w_dec)
+    )(place, x, gain, w_in, w_out, w_dec, observed, obs_count)
 
 
 def sum_over_groups(tile, width):
@@ -149,7 +203,7 @@
     return jnp.where(lanes_of(here.shape) < LANES - move, here, there)
 
 
-def pair_sums(fields, observed, prec, width, weighted, moved, put):
+def pair_sums(fields, prec, width, weighted, moved, put):
     count = len(fields)
     per = LANES // width
     total = fields[0]
@@ -165,42 +219,33 @@
     for t in range(1, per):
         for k in range(count):
             moved[t, k] = shifted_tile(lambda j: moved[0, j % count], k, t, width)
-    innovation = observed - mean
-    for k in range(count):
-        put(DIAGS, k, jnp.sum(weighted[k] * innovation, axis=0, keepdims=True))
     for s in range(DIAGS):
         on, t = divmod(s, per)
         for k in range(count):
             put(s, k, jnp.sum(weighted[k] * moved[t, (k + on) % count], axis=0, keepdims=True))
-    return anomalies
-
-
-def pairs_kernel(
-    recv_ref, west_ref, east_ref, err_ref, taper_ref, out_ref, anom_ref,
-    wide, weighted, moved, sums,
-):
+    return mean, anomalies
+
+
+def pairs_kernel(recv_ref, err_ref, sums, weighted, mean_ref, anom_ref, wide, moved):
     tiles = recv_ref.shape[0] // CORES
-    variables = west_ref.shape[2]
+    variables = err_ref.shape[0]
     wide[...] = jnp.zeros_like(wide)
     wide[0:1, 0:variables] = err_ref[...].reshape(1, variables)
     err = jnp.broadcast_to(wide[0:1, :], (LANES, LANES)).T[:VROWS]
     is_variable = lax.broadcasted_iota(jnp.int32, err.shape, 0) < variables
-    each = jnp.where(is_variable, COUNT / (err * err), 0.0)
-
+    prec = jnp.where(is_variable, COUNT / (err * err), 0.0)
+
+    sums[pl.ds(DIAGS * tiles, tiles), :] = jnp.zeros((tiles, CORES * LANES), F32)
     anomalies = []
     for r in range(CORES):
-        wide[0:HALF, 0:variables] = west_ref[r]
-        wide[HALF:WINDOW, 0:variables] = east_ref[r]
-        obs = jnp.concatenate([wide[...]] * GROUP, axis=0).T[:VROWS]
-        prec = jnp.where(obs < 0.5 * UNSEEN, each, 0.0)
 
         def put(s, k, row):
             sums[pl.ds(s * tiles + k, 1), r * LANES : (r + 1) * LANES] = row
 
         fields = [recv_ref[CORES * m + r].astype(F32) for m in range(tiles)]
-        anomalies.append(
-            pair_sums(fields, obs, prec, WINDOW, weighted.at[r], moved.at[r], put)
-        )
+        mean, anomaly = pair_sums(fields, prec, WINDOW, weighted.at[r], moved.at[r], put)
+        mean_ref[r] = mean
+        anomalies.append(anomaly)
     lower = lanes_of((VROWS, LANES)) % POINTS < HALF
     for k in range(tiles):
         anom_ref[k] = jnp.where(
@@ -208,6 +253,24 @@
             pltpu.roll(anomalies[0][k], LANES - HALO, 1),
             pltpu.roll(anomalies[1][k], HALF - HALO, 1),
         )
+
+
+def smooth_kernel(sums_ref, weighted, mean_ref, west_ref, east_ref, taper_ref, out_ref, wide, sums):
+    tiles = weighted.shape[1]
+    variables = west_ref.shape[2]
+    wide[...] = jnp.zeros_like(wide)
+    for r in range(CORES):
+        at = slice(r * LANES, (r + 1) * LANES)
+        wide[0:HALF, 0:variables] = west_ref[r]
+        wide[HALF:WINDOW, 0:variables] = east_ref[r]
+        obs = jnp.concatenate([wide[...]] * GROUP, axis=0).T[:VROWS]
+        is_seen = obs[0:1] < 0.5 * UNSEEN
+        innovation = obs - mean_ref[r]
+        diags = sums_ref[0 : DIAGS * tiles, at]
+        sums[0 : DIAGS * tiles, at] = jnp.where(is_seen, diags, 0.0)
+        for k in range(tiles):
+            row = jnp.sum(weighted[r, k] * innovation, axis=0, keepdims=True)
+            sums[pl.ds(DIAGS * tiles + k, 1), at] = jnp.where(is_seen, row, 0.0)
     smooth = jnp.dot(
         sums[...], taper_ref[...], precision=lax.Precision.HIGHEST, preferred_element_type=F32
     ).astype(BF16)
@@ -231,26 +294,39 @@
     return jnp.asarray(np.where(same, weight, 0.0).astype(np.float32))
 
 
-def pairs(recv, obs, err, chips):
+def pairs(recv, err):
     tiles = recv.shape[0] // CORES
     full = pl.BlockSpec(memory_space=pltpu.VMEM)
     return pl.pallas_call(
         pairs_kernel,
-        in_specs=[full] * 5,
-        out_specs=(full, full),
+        in_specs=[full] * 2,
+        out_specs=(full,) * 4,
         out_shape=(
-            jax.ShapeDtypeStruct((chips, ROWS * tiles, LANES), BF16),
+            jax.ShapeDtypeStruct((ROWS * tiles, CORES * LANES), F32),
+            jax.ShapeDtypeStruct((CORES, tiles, VROWS, LANES), F32),
+            jax.ShapeDtypeStruct((CORES, VROWS, LANES), F32),
             jax.ShapeDtypeStruct((tiles, VROWS, LANES), F32),
         ),
         scratch_shapes=[
-            pltpu.VMEM((WINDOW, LANES), F32),
-            pltpu.VMEM((CORES, tiles, VROWS, LANES), F32),
+            pltpu.VMEM((8, LANES), F32),
             pltpu.VMEM((CORES, LANES // WINDOW, tiles, VROWS, LANES), F32),
-            pltpu.VMEM((ROWS * tiles, CORES * LANES), F32),
         ],
         compiler_params=SMALL,
         name="pairs",
-    )(recv, *obs, err, longitude_taper())
+    )(recv, err)
+
+
+def smooth(sums, weighted, mean, obs, chips):
+    full = pl.BlockSpec(memory_space=pltpu.VMEM)
+    return pl.pallas_call(
+        smooth_kernel,
+        in_specs=[full] * 6,
+        out_specs=full,
+        out_shape=jax.ShapeDtypeStruct((chips, sums.shape[0], LANES), BF16),
+        scratch_shapes=[pltpu.VMEM((WINDOW, LANES), F32), pltpu.VMEM(sums.shape, F32)],
+        compiler_params=SMALL,
+        name="smooth",
+    )(sums, weighted, mean, *obs, longitude_taper())
 
 
 def on_by(x, n):
@@ -429,35 +505,42 @@
     n_mem, n_tile = lax.axis_size("mem"), lax.axis_size("tile")
     chips = n_tile // CORES
     mem, tile = lax.axis_index("mem"), lax.axis_index("tile")
-    place = lax.div(tile, CORES).astype(jnp.int32).reshape(1)
+    chip_place = lax.div(tile, CORES).astype(jnp.int32).reshape(1)
+    place = lax.axis_index(("mem", "tile")).astype(jnp.int32).reshape(1)
+    n_y = n_mem // 2
     by_chip = [
         [m * n_tile + c * CORES + k for m in range(n_mem) for k in range(CORES)] for c in range(chips)
     ]
     by_core = [[c * CORES + k for c in range(chips)] for k in range(CORES)]
 
-    seen = jnp.where(obs_count > 0, observed, UNSEEN)
-    seen = lax.dynamic_slice_in_dim(seen, CORES * mem, CORES, 2)
-    seen = jnp.transpose(seen, (2, 1, 0))
-
-    def to_sector(part, move):
-        pairs_of = []
-        for m in range(n_mem):
-            for j in range(n_tile):
-                to = (j + move) % n_tile
-                pairs_of.append((m * n_tile + j, to // CORES * n_tile + CORES * m + to % CORES))
-        return lax.ppermute(part, ("mem", "tile"), pairs_of)
-
-    obs = [to_sector(seen, 0), to_sector(seen, -1)]
-
-    fields = forecast(
-        hidden_in.reshape(mem_dev * tok_dev, width), norm_gain, w_in, w_out, w_dec
+    fields, *seen = forecast(
+        place,
+        n_y,
+        hidden_in.reshape(mem_dev * tok_dev, width),
+        norm_gain,
+        w_in,
+        w_out,
+        w_dec,
+        jnp.transpose(observed, (1, 2, 0)),
+        jnp.transpose(obs_count, (1, 2, 0)),
     )
     halves = lax.all_to_all(
         fields, ("mem", "tile"), 0, 0, tiled=True, axis_index_groups=by_chip
     )
-    smooth, anomaly = pairs(halves, obs, obs_error, chips)
-    rows = lax.all_to_all(smooth, "tile", 0, 0, tiled=True, axis_index_groups=by_core)
-    increments = transform(place, rows, anomaly)
+
+    mems, tiles = np.divmod(np.arange(n_mem * n_tile), n_tile)
+    obs = []
+    for k, move in enumerate(SENDS):
+        targets = []
+        for m, t in zip(mems.tolist(), tiles.tolist()):
+            half, chip = served_here(m, t, move, (n_tile, n_y))
+            targets.append((m * n_tile + t, half // CORES * n_tile + CORES * chip + half % CORES))
+        obs.append(lax.ppermute(seen[k], ("mem", "tile"), targets))
+
+    sums, weighted, mean, anomaly = pairs(halves, obs_error)
+    smoothed = smooth(sums, weighted, mean, obs, chips)
+    rows = lax.all_to_all(smoothed, "tile", 0, 0, tiled=True, axis_index_groups=by_core)
+    increments = transform(chip_place, rows, anomaly)
     back = lax.all_to_all(
         increments, ("mem", "tile"), 0, 0, tiled=True, axis_index_groups=by_chip
     )

time: 81.3 us -> 76.2 us (0.937)
  blocking collectives: 13.1 us -> 9.04 us
  waiting for transfers between devices: 12.9 us -> 10.9 us
  starting transfers between devices: 19.9 us -> 21.6 us
  local copies, waits for them, and re-layouts: 0.88 us -> 0.01 us
    ppermute x2, starting transfers between devices: 1.01 us -> 6.72 us  [body(): obs.append(lax.ppermute(seen[k], ('mem', 'tile'), targets))]
    all_to_all x1, blocking collectives: 13.1 us -> 9.04 us  [body(): lax.all_to_all(increments, ('mem', 'tile'), 0, 0, tiled=True, axis_index_...]
    all_to_all x1, starting transfers between devices: 11.5 us -> 7.56 us  [body(): lax.all_to_all(smoothed, 'tile', 0, 0, tiled=True, axis_index_groups=by_c...]
    ppermute x2, waiting for transfers between devices: 4.08 us -> 1.94 us  [body(): obs.append(lax.ppermute(seen[k], ('mem', 'tile'), targets))]
    dynamic_slice x2 -> x0, local copies, waits for them, and re-layouts: 0.87 us -> none  [body(): seen = lax.dynamic_slice_in_dim(seen, CORES * mem, CORES, 2)]
    all_to_all x1, waiting for transfers between devices: 7.42 us -> 8.26 us  [body(): lax.all_to_all(smoothed, 'tile', 0, 0, tiled=True, axis_index_groups=by_c...]
    pallas_call x2 -> x3, Pallas kernels: 28 us -> 28.2 us  [the longest x1 25.6 us: forecast(): pl.pallas_call(functools.partial(forecast_kernel, n_y=n_y), grid=(hidden...]
  transfers between devices with their start and end apart: 4 -> 4, of which waited for: 3 -> 3; matrix products, arithmetic and copies ran while one was open for 1% -> 0% of each run, Pallas kernels for 0% -> 2%
where the time goes in v3:
time: 76.2 us; the launch traced here: 75.8 us
  Pallas kernels  34.3 us (45%)
  starting transfers between devices  21.6 us (28%)
  waiting for transfers between devices  10.9 us (14%)
  blocking collectives  9.04 us (12%)
    pallas_call x1, Pallas kernels, forecast(): pl.pallas_call(functools.partial(forecast_kernel, n_y=n_y), grid=(hidden...  25.6 us
    all_to_all x1, blocking collectives, body(): lax.all_to_all(increments, ('mem', 'tile'), 0, 0, tiled=True, axis_index_...  9.04 us
    all_to_all x1, waiting for transfers between devices, body(): lax.all_to_all(smoothed, 'tile', 0, 0, tiled=True, axis_index_groups=by_c...  8.26 us
    all_to_all x1, starting transfers between devices, body(): lax.all_to_all(smoothed, 'tile', 0, 0, tiled=True, axis_index_groups=by_c...  7.56 us
    all_to_all x1, starting transfers between devices, body(): lax.all_to_all(fields, ('mem', 'tile'), 0, 0, tiled=True, axis_index_grou...  7.33 us
    ppermute x2, starting transfers between devices, body(): obs.append(lax.ppermute(seen[k], ('mem', 'tile'), targets))  6.72 us
    pallas_call x1, Pallas kernels, transform(): pl.pallas_call(transform_kernel, in_specs=[pl.BlockSpec(memory_space=pltp...  4.92 us
    ppermute x2, waiting for transfers between devices, body(): obs.append(lax.ppermute(seen[k], ('mem', 'tile'), targets))  1.94 us
  transfers between devices with their start and end apart: 4, of which 3 were waited for; matrix products, arithmetic and copies ran while one was open for 0% of the time, Pallas kernels for 2%

profile of v3, /device:TPU:1, one launch (start us, length us, event | category | flops | bytes accessed | tf_op | source)
XLA Modules:
  0.0 75.8 jit_solution(10998294743583575550)
XLA Ops:
  0.0 0.0 copy-start.1
  0.0 0.0 copy-start
  0.0 25.6 %forecast.1 = (bf16[16,72,128]{2,1,0:T(8,128)(2,1)}, f32[2,16,69]{2,1,0:T(8,128)}, f32[2,16,69]{2,1,0:T(8,128)}) custom-call(s32[1]{0:T(128)} %bitcast.1.place_ref, bf16[1024,1024]{1,0:T(8,128)(2,1)} %bitcast.5, bf16[1024]{0:T(1024)(128)(2,1)} %gain_ref.1, bf16[1024,4096]{1,0:T(8,128)(2,1)} %win_ref.1, bf16[4096,1024]{1,0:T(8,128)(2,1)} %wout_ref.1, ...), custom_call_target="tpu_custom_call" | custom-call | flops 17179869184 | bytes 16777216 | tf_op jit(solution)/shard_map/forecast/pallas_call | solution.py:154
  25.6 7.3 %all-to-all-start = ((bf16[16,72,128]{2,1,0:T(8,128)(2,1)}), bf16[16,72,128]{2,1,0:T(8,128)(2,1)S(1)}, u32[]{:S(2)}, u32[]{:S(2)}) async-start(bf16[16,72,128]{2,1,0:T(8,128)(2,1)} %get-tuple-element.12), calls=%async_computation | async-start | bytes 589824 | tf_op jit(solution)/shard_map/all_to_all | solution.py:527
  32.9 2.7 %collective-permute-start = (f32[2,16,69]{2,1,0:T(8,128)}, f32[2,16,69]{2,1,0:T(8,128)S(1)}, u32[]{:S(2)}, u32[]{:S(2)}) collective-permute-start(f32[2,16,69]{2,1,0:T(8,128)} %get-tuple-element.16), channel_id=1, source_target_pairs={{0,8},{1,9},{2,30},{3,31},{4,36},{5,37},{6,58},{7,59},{8,66},{9,67... | collective-permute-start | bytes 26504 | tf_op jit(solution)/shard_map/ppermute | solution.py:538
  35.6 4.0 %collective-permute-start.1 = (f32[2,16,69]{2,1,0:T(8,128)}, f32[2,16,69]{2,1,0:T(8,128)S(1)}, u32[]{:S(2)}, u32[]{:S(2)}) collective-permute-start(f32[2,16,69]{2,1,0:T(8,128)} %get-tuple-element.17), channel_id=1, source_target_pairs={{0,119},{1,8},{2,11},{3,30},{4,17},{5,36},{6,39},{7,58},{8,61},{9,... | collective-permute-start | bytes 26504 | tf_op jit(solution)/shard_map/ppermute | solution.py:538
  39.6 0.7 all-to-all-done.recv_ref
  40.3 0.0 copy-done.1
  40.3 1.6 %pairs.1 = (f32[144,256]{1,0:T(8,128)S(1)}, f32[2,8,72,128]{3,2,1,0:T(8,128)S(1)}, f32[2,72,128]{2,1,0:T(8,128)S(1)}, f32[8,72,128]{2,1,0:T(8,128)S(1)}) custom-call(bf16[16,72,128]{2,1,0:T(8,128)(2,1)S(1)} %all-to-all-done.recv_ref, f32[69]{0:T(128)S(1)} %copy-done.1), custom_call_target="tpu_custom_call" | custom-call | tf_op jit(solution)/shard_map/pairs/pallas_call | solution.py:300
  41.9 0.0 collective-permute-done.west_ref
  41.9 1.9 %collective-permute-done.1.east_ref = f32[2,16,69]{2,1,0:T(8,128)S(1)} collective-permute-done((f32[2,16,69]{2,1,0:T(8,128)}, f32[2,16,69]{2,1,0:T(8,128)S(1)}, u32[]{:S(2)}, u32[]{:S(2)}) %collective-permute-start.1) | collective-permute-done | bytes 8864 | tf_op jit(solution)/shard_map/ppermute | solution.py:538
  43.8 0.0 copy-done
  43.8 1.1 %smooth.1 = bf16[8,144,128]{2,1,0:T(8,128)(2,1)} custom-call(f32[144,256]{1,0:T(8,128)S(1)} %get-tuple-element.13.sums_ref, f32[2,8,72,128]{3,2,1,0:T(8,128)S(1)} %get-tuple-element.14.weighted, f32[2,72,128]{2,1,0:T(8,128)S(1)} %get-tuple-element.15.mean_ref, f32[2,16,69]{2,1,0:T(8,128)S(1)} %collective-permute-done.west_ref, ...), custom_call_target="tpu_custom_call" | custom-call | tf_op jit(solution)/shard_map/smooth/pallas_call | solution.py:321
  44.9 7.6 %all-to-all-start.1 = ((bf16[8,144,128]{2,1,0:T(8,128)(2,1)}), bf16[8,144,128]{2,1,0:T(8,128)(2,1)S(1)}, u32[]{:S(2)}, u32[]{:S(2)}) async-start(bf16[8,144,128]{2,1,0:T(8,128)(2,1)} %smooth.1), calls=%async_computation.1 | async-start | bytes 589824 | tf_op jit(solution)/shard_map/all_to_all | solution.py:542
  52.5 8.3 %all-to-all-done.1.recv_ref = bf16[8,144,128]{2,1,0:T(8,128)(2,1)S(1)} async-done(((bf16[8,144,128]{2,1,0:T(8,128)(2,1)}), bf16[8,144,128]{2,1,0:T(8,128)(2,1)S(1)}, u32[]{:S(2)}, u32[]{:S(2)}) %all-to-all-start.1) | async-done | bytes 294944 | tf_op jit(solution)/shard_map/all_to_all | solution.py:542
  60.8 4.9 %transform.1 = bf16[16,40,128]{2,1,0:T(8,128)(2,1)S(1)} custom-call(s32[1]{0:T(128)} %bitcast.place_ref, bf16[8,144,128]{2,1,0:T(8,128)(2,1)S(1)} %all-to-all-done.1.recv_ref, f32[8,72,128]{2,1,0:T(8,128)S(1)} %get-tuple-element.18.anom_ref), custom_call_target="tpu_custom_call" | custom-call | tf_op jit(solution)/shard_map/transform/pallas_call | solution.py:446
  65.7 9.0 %all_to_all.15.recv_ref = bf16[16,40,128]{2,1,0:T(8,128)(2,1)S(1)} all-to-all(bf16[16,40,128]{2,1,0:T(8,128)(2,1)S(1)} %transform.1), channel_id=1, replica_groups={{0,1,16,17,32,33,48,49,64,65,80,81,96,97,112,113},{2,3,18,19,34,35,50,5..., dimensions={0} | all-to-all | bytes 327680 | tf_op jit(solution)/shard_map/all_to_all | solution.py:544
  74.7 1.1 %strips.1 = f32[4,69,1,256]{3,2,1,0:T(1,128)} custom-call(bf16[16,40,128]{2,1,0:T(8,128)(2,1)S(1)} %all_to_all.15.recv_ref), custom_call_target="tpu_custom_call" | custom-call | tf_op jit(solution)/shard_map/strips/pallas_call | solution.py:492
Async XLA Ops:
  0.0 40.3 %copy-start.1 = (f32[69]{0:T(128)S(1)}, f32[69]{0:T(128)}, u32[]{:S(2)}) copy-start(f32[69]{0:T(128)} %err_ref.1) | copy-start | bytes 832
  0.0 43.8 %copy-start = (f32[256,128]{1,0:T(8,128)S(1)}, f32[256,128]{1,0:T(8,128)}, u32[]{:S(2)}) copy-start(f32[256,128]{1,0:T(8,128)} %constant.18.clone.taper_ref) | copy-start | bytes 393220
  25.6 14.7 %all-to-all-start = ((bf16[16,72,128]{2,1,0:T(8,128)(2,1)}), bf16[16,72,128]{2,1,0:T(8,128)(2,1)S(1)}, u32[]{:S(2)}, u32[]{:S(2)}) async-start(bf16[16,72,128]{2,1,0:T(8,128)(2,1)} %get-tuple-element.12), calls=%async_computation | async-start | bytes 589824 | tf_op jit(solution)/shard_map/all_to_all | solution.py:527
  32.9 9.0 %collective-permute-start = (f32[2,16,69]{2,1,0:T(8,128)}, f32[2,16,69]{2,1,0:T(8,128)S(1)}, u32[]{:S(2)}, u32[]{:S(2)}) collective-permute-start(f32[2,16,69]{2,1,0:T(8,128)} %get-tuple-element.16), channel_id=1, source_target_pairs={{0,8},{1,9},{2,30},{3,31},{4,36},{5,37},{6,58},{7,59},{8,66},{9,67... | collective-permute-start | bytes 26504 | tf_op jit(solution)/shard_map/ppermute | solution.py:538
  35.6 8.2 %collective-permute-start.1 = (f32[2,16,69]{2,1,0:T(8,128)}, f32[2,16,69]{2,1,0:T(8,128)S(1)}, u32[]{:S(2)}, u32[]{:S(2)}) collective-permute-start(f32[2,16,69]{2,1,0:T(8,128)} %get-tuple-element.17), channel_id=1, source_target_pairs={{0,119},{1,8},{2,11},{3,30},{4,17},{5,36},{6,39},{7,58},{8,61},{9,... | collective-permute-start | bytes 26504 | tf_op jit(solution)/shard_map/ppermute | solution.py:538
  44.9 15.8 %all-to-all-start.1 = ((bf16[8,144,128]{2,1,0:T(8,128)(2,1)}), bf16[8,144,128]{2,1,0:T(8,128)(2,1)S(1)}, u32[]{:S(2)}, u32[]{:S(2)}) async-start(bf16[8,144,128]{2,1,0:T(8,128)(2,1)} %smooth.1), calls=%async_computation.1 | async-start | bytes 589824 | tf_op jit(solution)/shard_map/all_to_all | solution.py:542

commit v4 on v3

--- a/solution.py
+++ b/solution.py
@@ -132,17 +132,19 @@
 
     @pl.when(step == steps - 1)
     def _():
-        acc[...] = x_ref[...].astype(F32) + acc[...]
         wdec = decoder[...]
         contract = (((1,), (1,)), ((), ()))
+        for r in range(blocks):
+            at = pl.ds(r * TOKEN_BLOCK, TOKEN_BLOCK)
+            layer_out = (x_ref[at, :].astype(F32) + acc[at, :]).astype(BF16)
+            fields = lax.dot_general(layer_out, wdec, contract, preferred_element_type=F32)
+            acc[at, 0 : 2 * HROWS] = fields
         for h in range(lon_all // HALF):
             window = []
             for m in range(GROUP):
                 for at in (HALF * h, HALF * (h + 1)):
-                    window.append(acc[pl.ds(m * lon_all + at % lon_all, HALF), :])
-            window = jnp.concatenate(window, axis=0).astype(BF16)
-            decoded = lax.dot_general(wdec, window, contract, preferred_element_type=F32)
-            out_ref[h] = decoded[:VROWS].astype(BF16)
+                    window.append(acc[pl.ds(m * lon_all + at % lon_all, HALF), 0:LANES])
+            out_ref[h] = jnp.concatenate(window, axis=0).T[:VROWS].astype(BF16)
 
 
 def forecast(place, n_y, x, gain, w_in, w_out, w_dec, observed, obs_count):
@@ -351,9 +353,24 @@
     return total
 
 
-def product(left, right, out, scale=None, shift=None):
+def spread(right, turned):
+    for u in range(MEMBERS):
+        value = right[u]
+        for a in range(MEMBERS // GROUP):
+            turned[a, u] = on_by(value, GROUP * a)
+
+
+def product(left, turned, out, scale=None, shift=None):
+    moved = [on_by(left[(-t) % MEMBERS], t // GROUP * GROUP) for t in range(MEMBERS)]
     for s in range(DIAGS):
-        value = shifted_sum(lambda t: left[(-t) % MEMBERS] * right[(s - t) % MEMBERS])
+        value = None
+        for t in range(GROUP - 1, -1, -1):
+            parts = [
+                moved[at] * turned[at // GROUP, (s - at) % MEMBERS] for at in range(t, MEMBERS, GROUP)
+            ]
+            while len(parts) > 1:
+                parts = [a + b for a, b in zip(parts[::2], parts[1::2])]
+            value = parts[0] if value is None else on_by(value, 1) + parts[0]
         if scale is not None:
             value = scale * value
             if s == 0:
@@ -372,7 +389,7 @@
     return jnp.where(jnp.abs(offset) <= RAD, (1.0 - ratio * ratio) * (1.0 - ratio * ratio), 0.0)
 
 
-def transform_kernel(place_ref, recv_ref, anom_ref, out_ref, bank, moved, coeff):
+def transform_kernel(place_ref, recv_ref, anom_ref, out_ref, bank, turned, moved, coeff):
     chips = recv_ref.shape[0]
     tiles = anom_ref.shape[0]
     same, south, north = None, None, None
@@ -407,12 +424,15 @@
     mirror(gram)
     for s in range(MEMBERS):
         inv_root[s] = -0.5 * gram[s] + (1.5 if s == 0 else 0.0)
-    product(gram, inv_root, root)
+    spread(inv_root, turned)
+    product(gram, turned, root)
     for sweep in range(1, NS_ITERS):
-        product(inv_root, root, corr, -0.5, 1.5)
+        spread(root, turned)
+        product(inv_root, turned, corr, -0.5, 1.5)
+        spread(corr, turned)
         if sweep < NS_ITERS - 1:
-            product(root, corr, other_root)
-        product(corr, inv_root, other_inv)
+            product(root, turned, other_root)
+        product(inv_root, turned, other_inv)
         root, other_root = other_root, root
         inv_root, other_inv = other_inv, inv_root
     half = shifted_sum(lambda t: inv_root[(-t) % MEMBERS] * innov)
@@ -427,12 +447,13 @@
         for k in range(tiles):
             moved[t, k] = shifted_tile(lambda j: moved[0, j % tiles], k, t, POINTS)
     for k in range(tiles):
-        mixed = None
-        for s in range(MEMBERS):
-            on, t = divmod(s, GROUP)
-            part = moved[t, (k + on) % tiles] * coeff[pl.ds(s * tiles + k, 1), :]
-            mixed = part if mixed is None else mixed + part
-        mixed = mixed - anom_ref[k]
+        mixed = -anom_ref[k]
+        for on in range(tiles):
+            parts = [
+                moved[t, (k + on) % tiles] * coeff[pl.ds((GROUP * on + t) * tiles + k, 1), :]
+                for t in range(GROUP)
+            ]
+            mixed = mixed + ((parts[0] + parts[1]) + (parts[2] + parts[3]))
         low = mixed[:HROWS]
         high = jnp.concatenate([mixed[HROWS:], jnp.zeros((2 * HROWS - VROWS, LANES), F32)], axis=0)
         first = lanes_of(low.shape) % POINTS < HALF
@@ -450,6 +471,7 @@
         out_shape=jax.ShapeDtypeStruct((CORES * tiles, HROWS, LANES), BF16),
         scratch_shapes=[
             pltpu.VMEM((6, MEMBERS, tiles, LANES), F32),
+            pltpu.VMEM((MEMBERS // GROUP, MEMBERS, tiles, LANES), F32),
             pltpu.VMEM((GROUP, tiles, VROWS, LANES), F32),
             pltpu.VMEM((MEMBERS * tiles, LANES), F32),
         ],

time: 76.2 us -> 75 us (0.984)
  Pallas kernels: 34.3 us -> 33.1 us
where the time goes in v4:
time: 75 us; the launch traced here: 74.6 us
  Pallas kernels  33.1 us (44%)
  starting transfers between devices  21.6 us (29%)
  waiting for transfers between devices  10.9 us (15%)
  blocking collectives  9.03 us (12%)
    pallas_call x1, Pallas kernels, forecast(): pl.pallas_call(functools.partial(forecast_kernel, n_y=n_y), grid=(hidden...  24.8 us
    all_to_all x1, blocking collectives, body(): lax.all_to_all(increments, ('mem', 'tile'), 0, 0, tiled=True, axis_index_...  9.03 us
    all_to_all x1, waiting for transfers between devices, body(): lax.all_to_all(smoothed, 'tile', 0, 0, tiled=True, axis_index_groups=by_c...  8.27 us
    all_to_all x1, starting transfers between devices, body(): lax.all_to_all(smoothed, 'tile', 0, 0, tiled=True, axis_index_groups=by_c...  7.56 us
    all_to_all x1, starting transfers between devices, body(): lax.all_to_all(fields, ('mem', 'tile'), 0, 0, tiled=True, axis_index_grou...  7.33 us
    ppermute x2, starting transfers between devices, body(): obs.append(lax.ppermute(seen[k], ('mem', 'tile'), targets))  6.72 us
    pallas_call x1, Pallas kernels, transform(): pl.pallas_call(transform_kernel, in_specs=[pl.BlockSpec(memory_space=pltp...  4.46 us
    ppermute x2, waiting for transfers between devices, body(): obs.append(lax.ppermute(seen[k], ('mem', 'tile'), targets))  1.94 us
  transfers between devices with their start and end apart: 4, of which 3 were waited for; matrix products, arithmetic and copies ran while one was open for 0% of the time, Pallas kernels for 2%

profile of v4, /device:TPU:1, one launch (start us, length us, event | category | flops | bytes accessed | tf_op | source)
XLA Modules:
  0.0 74.6 jit_solution(16906384231378574657)
XLA Ops:
  0.0 0.0 copy-start.1
  0.0 0.0 copy-start
  0.0 24.8 %forecast.1 = (bf16[16,72,128]{2,1,0:T(8,128)(2,1)}, f32[2,16,69]{2,1,0:T(8,128)}, f32[2,16,69]{2,1,0:T(8,128)}) custom-call(s32[1]{0:T(128)} %bitcast.1.place_ref, bf16[1024,1024]{1,0:T(8,128)(2,1)} %bitcast.5, bf16[1024]{0:T(1024)(128)(2,1)} %gain_ref.1, bf16[1024,4096]{1,0:T(8,128)(2,1)} %win_ref.1, bf16[4096,1024]{1,0:T(8,128)(2,1)} %wout_ref.1, ...), custom_call_target="tpu_custom_call" | custom-call | flops 17179869184 | bytes 16777216 | tf_op jit(solution)/shard_map/forecast/pallas_call | solution.py:156
  24.8 7.3 %all-to-all-start = ((bf16[16,72,128]{2,1,0:T(8,128)(2,1)}), bf16[16,72,128]{2,1,0:T(8,128)(2,1)S(1)}, u32[]{:S(2)}, u32[]{:S(2)}) async-start(bf16[16,72,128]{2,1,0:T(8,128)(2,1)} %get-tuple-element.12), calls=%async_computation | async-start | bytes 589824 | tf_op jit(solution)/shard_map/all_to_all | solution.py:549
  32.2 2.7 %collective-permute-start = (f32[2,16,69]{2,1,0:T(8,128)}, f32[2,16,69]{2,1,0:T(8,128)S(1)}, u32[]{:S(2)}, u32[]{:S(2)}) collective-permute-start(f32[2,16,69]{2,1,0:T(8,128)} %get-tuple-element.16), channel_id=1, source_target_pairs={{0,8},{1,9},{2,30},{3,31},{4,36},{5,37},{6,58},{7,59},{8,66},{9,67... | collective-permute-start | bytes 26504 | tf_op jit(solution)/shard_map/ppermute | solution.py:560
  34.9 4.0 %collective-permute-start.1 = (f32[2,16,69]{2,1,0:T(8,128)}, f32[2,16,69]{2,1,0:T(8,128)S(1)}, u32[]{:S(2)}, u32[]{:S(2)}) collective-permute-start(f32[2,16,69]{2,1,0:T(8,128)} %get-tuple-element.17), channel_id=1, source_target_pairs={{0,119},{1,8},{2,11},{3,30},{4,17},{5,36},{6,39},{7,58},{8,61},{9,... | collective-permute-start | bytes 26504 | tf_op jit(solution)/shard_map/ppermute | solution.py:560
  38.9 0.7 all-to-all-done.recv_ref
  39.6 0.0 copy-done.1
  39.6 1.6 %pairs.1 = (f32[144,256]{1,0:T(8,128)S(1)}, f32[2,8,72,128]{3,2,1,0:T(8,128)S(1)}, f32[2,72,128]{2,1,0:T(8,128)S(1)}, f32[8,72,128]{2,1,0:T(8,128)S(1)}) custom-call(bf16[16,72,128]{2,1,0:T(8,128)(2,1)S(1)} %all-to-all-done.recv_ref, f32[69]{0:T(128)S(1)} %copy-done.1), custom_call_target="tpu_custom_call" | custom-call | tf_op jit(solution)/shard_map/pairs/pallas_call | solution.py:302
  41.2 0.0 collective-permute-done.west_ref
  41.2 1.9 %collective-permute-done.1.east_ref = f32[2,16,69]{2,1,0:T(8,128)S(1)} collective-permute-done((f32[2,16,69]{2,1,0:T(8,128)}, f32[2,16,69]{2,1,0:T(8,128)S(1)}, u32[]{:S(2)}, u32[]{:S(2)}) %collective-permute-start.1) | collective-permute-done | bytes 8864 | tf_op jit(solution)/shard_map/ppermute | solution.py:560
  43.1 0.0 copy-done
  43.1 1.1 %smooth.1 = bf16[8,144,128]{2,1,0:T(8,128)(2,1)} custom-call(f32[144,256]{1,0:T(8,128)S(1)} %get-tuple-element.13.sums_ref, f32[2,8,72,128]{3,2,1,0:T(8,128)S(1)} %get-tuple-element.14.weighted, f32[2,72,128]{2,1,0:T(8,128)S(1)} %get-tuple-element.15.mean_ref, f32[2,16,69]{2,1,0:T(8,128)S(1)} %collective-permute-done.west_ref, ...), custom_call_target="tpu_custom_call" | custom-call | tf_op jit(solution)/shard_map/smooth/pallas_call | solution.py:323
  44.2 7.6 %all-to-all-start.1 = ((bf16[8,144,128]{2,1,0:T(8,128)(2,1)}), bf16[8,144,128]{2,1,0:T(8,128)(2,1)S(1)}, u32[]{:S(2)}, u32[]{:S(2)}) async-start(bf16[8,144,128]{2,1,0:T(8,128)(2,1)} %smooth.1), calls=%async_computation.1 | async-start | bytes 589824 | tf_op jit(solution)/shard_map/all_to_all | solution.py:564
  51.8 8.3 %all-to-all-done.1.recv_ref = bf16[8,144,128]{2,1,0:T(8,128)(2,1)S(1)} async-done(((bf16[8,144,128]{2,1,0:T(8,128)(2,1)}), bf16[8,144,128]{2,1,0:T(8,128)(2,1)S(1)}, u32[]{:S(2)}, u32[]{:S(2)}) %all-to-all-start.1) | async-done | bytes 294944 | tf_op jit(solution)/shard_map/all_to_all | solution.py:564
  60.0 4.5 %transform.1 = bf16[16,40,128]{2,1,0:T(8,128)(2,1)S(1)} custom-call(s32[1]{0:T(128)} %bitcast.place_ref, bf16[8,144,128]{2,1,0:T(8,128)(2,1)S(1)} %all-to-all-done.1.recv_ref, f32[8,72,128]{2,1,0:T(8,128)S(1)} %get-tuple-element.18.anom_ref), custom_call_target="tpu_custom_call" | custom-call | tf_op jit(solution)/shard_map/transform/pallas_call | solution.py:467
  64.5 9.0 %all_to_all.15.recv_ref = bf16[16,40,128]{2,1,0:T(8,128)(2,1)S(1)} all-to-all(bf16[16,40,128]{2,1,0:T(8,128)(2,1)S(1)} %transform.1), channel_id=1, replica_groups={{0,1,16,17,32,33,48,49,64,65,80,81,96,97,112,113},{2,3,18,19,34,35,50,5..., dimensions={0} | all-to-all | bytes 327680 | tf_op jit(solution)/shard_map/all_to_all | solution.py:566
  73.5 1.1 %strips.1 = f32[4,69,1,256]{3,2,1,0:T(1,128)} custom-call(bf16[16,40,128]{2,1,0:T(8,128)(2,1)S(1)} %all_to_all.15.recv_ref), custom_call_target="tpu_custom_call" | custom-call | tf_op jit(solution)/shard_map/strips/pallas_call | solution.py:514
Async XLA Ops:
  0.0 39.6 %copy-start.1 = (f32[69]{0:T(128)S(1)}, f32[69]{0:T(128)}, u32[]{:S(2)}) copy-start(f32[69]{0:T(128)} %err_ref.1) | copy-start | bytes 832
  0.0 43.1 %copy-start = (f32[256,128]{1,0:T(8,128)S(1)}, f32[256,128]{1,0:T(8,128)}, u32[]{:S(2)}) copy-start(f32[256,128]{1,0:T(8,128)} %constant.18.clone.taper_ref) | copy-start | bytes 393220
  24.8 14.7 %all-to-all-start = ((bf16[16,72,128]{2,1,0:T(8,128)(2,1)}), bf16[16,72,128]{2,1,0:T(8,128)(2,1)S(1)}, u32[]{:S(2)}, u32[]{:S(2)}) async-start(bf16[16,72,128]{2,1,0:T(8,128)(2,1)} %get-tuple-element.12), calls=%async_computation | async-start | bytes 589824 | tf_op jit(solution)/shard_map/all_to_all | solution.py:549
  32.2 9.0 %collective-permute-start = (f32[2,16,69]{2,1,0:T(8,128)}, f32[2,16,69]{2,1,0:T(8,128)S(1)}, u32[]{:S(2)}, u32[]{:S(2)}) collective-permute-start(f32[2,16,69]{2,1,0:T(8,128)} %get-tuple-element.16), channel_id=1, source_target_pairs={{0,8},{1,9},{2,30},{3,31},{4,36},{5,37},{6,58},{7,59},{8,66},{9,67... | collective-permute-start | bytes 26504 | tf_op jit(solution)/shard_map/ppermute | solution.py:560
  34.9 8.2 %collective-permute-start.1 = (f32[2,16,69]{2,1,0:T(8,128)}, f32[2,16,69]{2,1,0:T(8,128)S(1)}, u32[]{:S(2)}, u32[]{:S(2)}) collective-permute-start(f32[2,16,69]{2,1,0:T(8,128)} %get-tuple-element.17), channel_id=1, source_target_pairs={{0,119},{1,8},{2,11},{3,30},{4,17},{5,36},{6,39},{7,58},{8,61},{9,... | collective-permute-start | bytes 26504 | tf_op jit(solution)/shard_map/ppermute | solution.py:560
  44.2 15.8 %all-to-all-start.1 = ((bf16[8,144,128]{2,1,0:T(8,128)(2,1)}), bf16[8,144,128]{2,1,0:T(8,128)(2,1)S(1)}, u32[]{:S(2)}, u32[]{:S(2)}) async-start(bf16[8,144,128]{2,1,0:T(8,128)(2,1)} %smooth.1), calls=%async_computation.1 | async-start | bytes 589824 | tf_op jit(solution)/shard_map/all_to_all | solution.py:564

commit v5 on v4

--- a/solution.py
+++ b/solution.py
@@ -98,7 +98,7 @@
                 row = CORES * chip + r
                 seen_ref[r] = jnp.where(count_ref[:, row, :] > 0, obs_ref[:, row, :], UNSEEN)
         decoder[...] = jnp.zeros_like(decoder)
-        decoder[0 : wdec_ref.shape[0], :] = wdec_ref[...]
+        decoder[0 : wdec_ref.shape[0], :] = wdec_ref[...].astype(F32)
         for r in range(tokens // 128):
             xf = x_ref[pl.ds(r * 128, 128), :].astype(F32)
             centred = xf - jnp.mean(xf, axis=-1, keepdims=True)
@@ -132,7 +132,7 @@
 
     @pl.when(step == steps - 1)
     def _():
-        wdec = decoder[...]
+        wdec = decoder[...].astype(BF16)
         contract = (((1,), (1,)), ((), ()))
         for r in range(blocks):
             at = pl.ds(r * TOKEN_BLOCK, TOKEN_BLOCK)
@@ -179,7 +179,7 @@
         scratch_shapes=[
             pltpu.VMEM((tokens, width), BF16),
             pltpu.VMEM((tokens, width), F32),
-            pltpu.VMEM((2 * HROWS, width), BF16),
+            pltpu.VMEM((2 * HROWS, width), F32),
         ],
         compiler_params=LARGE,
         cost_estimate=pl.CostEstimate(
@@ -487,16 +487,21 @@
     parts = [recv_ref[h].astype(F32) for h in range(halves)]
     group = lax.rem(lanes_of(parts[0].shape) + (LANES - HALO), LANES) // HALF
     first = lanes_of(parts[0].shape) < HALO
+    held = lanes_of(parts[0].shape) // HALF
+    moved = []
+    for c in range(halves // per):
+        for way in range(per):
+            tile = parts[per * c + way]
+            for g in range(1, per):
+                tile = jnp.where(held == g, parts[per * c + (way + g) % per], tile)
+            moved.append(pltpu.roll(tile, (HALF * way + HALO) % LANES, 1))
     for m in range(GROUP):
         for side in range(2):
             tiles = []
             for c in range(halves // per):
                 tile = None
                 for j in range(per):
-                    piece = parts[per * c + j]
-                    move = (HALF * (j - side) - POINTS * m + HALO) % LANES
-                    if move:
-                        piece = pltpu.roll(piece, move, 1)
+                    piece = moved[per * c + (j - 2 * m - side) % per]
                     tile = piece if tile is None else jnp.where(group == j, piece, tile)
                 tiles.append(tile)
             for c in range(len(tiles)):

time: 75 us -> 74.9 us (level)
  no operation moved by 1% of the time
where the time goes in v5:
time: 74.9 us; the launch traced here: 74.6 us
  Pallas kernels  33 us (44%)
  starting transfers between devices  21.6 us (29%)
  waiting for transfers between devices  10.9 us (15%)
  blocking collectives  9.08 us (12%)
    pallas_call x1, Pallas kernels, forecast(): pl.pallas_call(functools.partial(forecast_kernel, n_y=n_y), grid=(hidden...  24.8 us
    all_to_all x1, blocking collectives, body(): lax.all_to_all(increments, ('mem', 'tile'), 0, 0, tiled=True, axis_index_...  9.08 us
    all_to_all x1, waiting for transfers between devices, body(): lax.all_to_all(smoothed, 'tile', 0, 0, tiled=True, axis_index_groups=by_c...  8.27 us
    all_to_all x1, starting transfers between devices, body(): lax.all_to_all(smoothed, 'tile', 0, 0, tiled=True, axis_index_groups=by_c...  7.53 us
    all_to_all x1, starting transfers between devices, body(): lax.all_to_all(fields, ('mem', 'tile'), 0, 0, tiled=True, axis_index_grou...  7.32 us
    ppermute x2, starting transfers between devices, body(): obs.append(lax.ppermute(seen[k], ('mem', 'tile'), targets))  6.74 us
    pallas_call x1, Pallas kernels, transform(): pl.pallas_call(transform_kernel, in_specs=[pl.BlockSpec(memory_space=pltp...  4.46 us
    ppermute x2, waiting for transfers between devices, body(): obs.append(lax.ppermute(seen[k], ('mem', 'tile'), targets))  1.96 us
  transfers between devices with their start and end apart: 4, of which 3 were waited for; matrix products, arithmetic and copies ran while one was open for 0% of the time, Pallas kernels for 2%

profile of v5, /device:TPU:1, one launch (start us, length us, event | category | flops | bytes accessed | tf_op | source)
XLA Modules:
  0.0 74.6 jit_solution(7680678490938465477)
XLA Ops:
  0.0 0.0 copy-start.1
  0.0 0.0 copy-start
  0.0 24.8 %forecast.1 = (bf16[16,72,128]{2,1,0:T(8,128)(2,1)}, f32[2,16,69]{2,1,0:T(8,128)}, f32[2,16,69]{2,1,0:T(8,128)}) custom-call(s32[1]{0:T(128)} %bitcast.1.place_ref, bf16[1024,1024]{1,0:T(8,128)(2,1)} %bitcast.5, bf16[1024]{0:T(1024)(128)(2,1)} %gain_ref.1, bf16[1024,4096]{1,0:T(8,128)(2,1)} %win_ref.1, bf16[4096,1024]{1,0:T(8,128)(2,1)} %wout_ref.1, ...), custom_call_target="tpu_custom_call" | custom-call | flops 17179869184 | bytes 16777216 | tf_op jit(solution)/shard_map/forecast/pallas_call | solution.py:156
  24.8 7.3 %all-to-all-start = ((bf16[16,72,128]{2,1,0:T(8,128)(2,1)}), bf16[16,72,128]{2,1,0:T(8,128)(2,1)S(1)}, u32[]{:S(2)}, u32[]{:S(2)}) async-start(bf16[16,72,128]{2,1,0:T(8,128)(2,1)} %get-tuple-element.12), calls=%async_computation | async-start | bytes 589824 | tf_op jit(solution)/shard_map/all_to_all | solution.py:554
  32.2 2.8 %collective-permute-start = (f32[2,16,69]{2,1,0:T(8,128)}, f32[2,16,69]{2,1,0:T(8,128)S(1)}, u32[]{:S(2)}, u32[]{:S(2)}) collective-permute-start(f32[2,16,69]{2,1,0:T(8,128)} %get-tuple-element.16), channel_id=1, source_target_pairs={{0,8},{1,9},{2,30},{3,31},{4,36},{5,37},{6,58},{7,59},{8,66},{9,67... | collective-permute-start | bytes 26504 | tf_op jit(solution)/shard_map/ppermute | solution.py:565
  34.9 4.0 %collective-permute-start.1 = (f32[2,16,69]{2,1,0:T(8,128)}, f32[2,16,69]{2,1,0:T(8,128)S(1)}, u32[]{:S(2)}, u32[]{:S(2)}) collective-permute-start(f32[2,16,69]{2,1,0:T(8,128)} %get-tuple-element.17), channel_id=1, source_target_pairs={{0,119},{1,8},{2,11},{3,30},{4,17},{5,36},{6,39},{7,58},{8,61},{9,... | collective-permute-start | bytes 26504 | tf_op jit(solution)/shard_map/ppermute | solution.py:565
  38.9 0.7 all-to-all-done.recv_ref
  39.6 0.0 copy-done.1
  39.6 1.6 %pairs.1 = (f32[144,256]{1,0:T(8,128)S(1)}, f32[2,8,72,128]{3,2,1,0:T(8,128)S(1)}, f32[2,72,128]{2,1,0:T(8,128)S(1)}, f32[8,72,128]{2,1,0:T(8,128)S(1)}) custom-call(bf16[16,72,128]{2,1,0:T(8,128)(2,1)S(1)} %all-to-all-done.recv_ref, f32[69]{0:T(128)S(1)} %copy-done.1), custom_call_target="tpu_custom_call" | custom-call | tf_op jit(solution)/shard_map/pairs/pallas_call | solution.py:302
  41.1 0.0 collective-permute-done.west_ref
  41.2 2.0 %collective-permute-done.1.east_ref = f32[2,16,69]{2,1,0:T(8,128)S(1)} collective-permute-done((f32[2,16,69]{2,1,0:T(8,128)}, f32[2,16,69]{2,1,0:T(8,128)S(1)}, u32[]{:S(2)}, u32[]{:S(2)}) %collective-permute-start.1) | collective-permute-done | bytes 8864 | tf_op jit(solution)/shard_map/ppermute | solution.py:565
  43.1 0.0 copy-done
  43.1 1.1 %smooth.1 = bf16[8,144,128]{2,1,0:T(8,128)(2,1)} custom-call(f32[144,256]{1,0:T(8,128)S(1)} %get-tuple-element.13.sums_ref, f32[2,8,72,128]{3,2,1,0:T(8,128)S(1)} %get-tuple-element.14.weighted, f32[2,72,128]{2,1,0:T(8,128)S(1)} %get-tuple-element.15.mean_ref, f32[2,16,69]{2,1,0:T(8,128)S(1)} %collective-permute-done.west_ref, ...), custom_call_target="tpu_custom_call" | custom-call | tf_op jit(solution)/shard_map/smooth/pallas_call | solution.py:323
  44.2 7.5 %all-to-all-start.1 = ((bf16[8,144,128]{2,1,0:T(8,128)(2,1)}), bf16[8,144,128]{2,1,0:T(8,128)(2,1)S(1)}, u32[]{:S(2)}, u32[]{:S(2)}) async-start(bf16[8,144,128]{2,1,0:T(8,128)(2,1)} %smooth.1), calls=%async_computation.1 | async-start | bytes 589824 | tf_op jit(solution)/shard_map/all_to_all | solution.py:569
  51.8 8.3 %all-to-all-done.1.recv_ref = bf16[8,144,128]{2,1,0:T(8,128)(2,1)S(1)} async-done(((bf16[8,144,128]{2,1,0:T(8,128)(2,1)}), bf16[8,144,128]{2,1,0:T(8,128)(2,1)S(1)}, u32[]{:S(2)}, u32[]{:S(2)}) %all-to-all-start.1) | async-done | bytes 294944 | tf_op jit(solution)/shard_map/all_to_all | solution.py:569
  60.0 4.5 %transform.1 = bf16[16,40,128]{2,1,0:T(8,128)(2,1)S(1)} custom-call(s32[1]{0:T(128)} %bitcast.place_ref, bf16[8,144,128]{2,1,0:T(8,128)(2,1)S(1)} %all-to-all-done.1.recv_ref, f32[8,72,128]{2,1,0:T(8,128)S(1)} %get-tuple-element.18.anom_ref), custom_call_target="tpu_custom_call" | custom-call | tf_op jit(solution)/shard_map/transform/pallas_call | solution.py:467
  64.5 9.1 %all_to_all.15.recv_ref = bf16[16,40,128]{2,1,0:T(8,128)(2,1)S(1)} all-to-all(bf16[16,40,128]{2,1,0:T(8,128)(2,1)S(1)} %transform.1), channel_id=1, replica_groups={{0,1,16,17,32,33,48,49,64,65,80,81,96,97,112,113},{2,3,18,19,34,35,50,5..., dimensions={0} | all-to-all | bytes 327680 | tf_op jit(solution)/shard_map/all_to_all | solution.py:571
  73.6 1.1 %strips.1 = f32[4,69,1,256]{3,2,1,0:T(1,128)} custom-call(bf16[16,40,128]{2,1,0:T(8,128)(2,1)S(1)} %all_to_all.15.recv_ref), custom_call_target="tpu_custom_call" | custom-call | tf_op jit(solution)/shard_map/strips/pallas_call | solution.py:519
Async XLA Ops:
  0.0 39.6 %copy-start.1 = (f32[69]{0:T(128)S(1)}, f32[69]{0:T(128)}, u32[]{:S(2)}) copy-start(f32[69]{0:T(128)} %err_ref.1) | copy-start | bytes 832
  0.0 43.1 %copy-start = (f32[256,128]{1,0:T(8,128)S(1)}, f32[256,128]{1,0:T(8,128)}, u32[]{:S(2)}) copy-start(f32[256,128]{1,0:T(8,128)} %constant.18.clone.taper_ref) | copy-start | bytes 393220
  24.8 14.7 %all-to-all-start = ((bf16[16,72,128]{2,1,0:T(8,128)(2,1)}), bf16[16,72,128]{2,1,0:T(8,128)(2,1)S(1)}, u32[]{:S(2)}, u32[]{:S(2)}) async-start(bf16[16,72,128]{2,1,0:T(8,128)(2,1)} %get-tuple-element.12), calls=%async_computation | async-start | bytes 589824 | tf_op jit(solution)/shard_map/all_to_all | solution.py:554
  32.2 9.0 %collective-permute-start = (f32[2,16,69]{2,1,0:T(8,128)}, f32[2,16,69]{2,1,0:T(8,128)S(1)}, u32[]{:S(2)}, u32[]{:S(2)}) collective-permute-start(f32[2,16,69]{2,1,0:T(8,128)} %get-tuple-element.16), channel_id=1, source_target_pairs={{0,8},{1,9},{2,30},{3,31},{4,36},{5,37},{6,58},{7,59},{8,66},{9,67... | collective-permute-start | bytes 26504 | tf_op jit(solution)/shard_map/ppermute | solution.py:565
  34.9 8.2 %collective-permute-start.1 = (f32[2,16,69]{2,1,0:T(8,128)}, f32[2,16,69]{2,1,0:T(8,128)S(1)}, u32[]{:S(2)}, u32[]{:S(2)}) collective-permute-start(f32[2,16,69]{2,1,0:T(8,128)} %get-tuple-element.17), channel_id=1, source_target_pairs={{0,119},{1,8},{2,11},{3,30},{4,17},{5,36},{6,39},{7,58},{8,61},{9,... | collective-permute-start | bytes 26504 | tf_op jit(solution)/shard_map/ppermute | solution.py:565
  44.2 15.8 %all-to-all-start.1 = ((bf16[8,144,128]{2,1,0:T(8,128)(2,1)}), bf16[8,144,128]{2,1,0:T(8,128)(2,1)S(1)}, u32[]{:S(2)}, u32[]{:S(2)}) async-start(bf16[8,144,128]{2,1,0:T(8,128)(2,1)} %smooth.1), calls=%async_computation.1 | async-start | bytes 589824 | tf_op jit(solution)/shard_map/all_to_all | solution.py:569

commit v6 on v5

--- a/solution.py
+++ b/solution.py
@@ -257,6 +257,11 @@
         )
 
 
+def two_parts(x):
+    high = x.astype(BF16)
+    return high, (x - high.astype(F32)).astype(BF16)
+
+
 def smooth_kernel(sums_ref, weighted, mean_ref, west_ref, east_ref, taper_ref, out_ref, wide, sums):
     tiles = weighted.shape[1]
     variables = west_ref.shape[2]
@@ -273,9 +278,11 @@
         for k in range(tiles):
             row = jnp.sum(weighted[r, k] * innovation, axis=0, keepdims=True)
             sums[pl.ds(DIAGS * tiles + k, 1), at] = jnp.where(is_seen, row, 0.0)
-    smooth = jnp.dot(
-        sums[...], taper_ref[...], precision=lax.Precision.HIGHEST, preferred_element_type=F32
-    ).astype(BF16)
+    high, low = two_parts(sums[...])
+    taper_high, taper_low = two_parts(taper_ref[...])
+    smooth = jnp.dot(high, taper_low, preferred_element_type=F32)
+    smooth = smooth + jnp.dot(low, taper_high, preferred_element_type=F32)
+    smooth = (smooth + jnp.dot(high, taper_high, preferred_element_type=F32)).astype(BF16)
     for c in range(out_ref.shape[0]):
         out_ref[c] = smooth
 

time: 74.9 us -> 74.9 us (level)
  no operation moved by 1% of the time
where the time goes in v6:
time: 74.9 us; the launch traced here: 74.6 us
  Pallas kernels  33 us (44%)
  starting transfers between devices  21.6 us (29%)
  waiting for transfers between devices  10.9 us (15%)
  blocking collectives  9.08 us (12%)
    pallas_call x1, Pallas kernels, forecast(): pl.pallas_call(functools.partial(forecast_kernel, n_y=n_y), grid=(hidden...  24.8 us
    all_to_all x1, blocking collectives, body(): lax.all_to_all(increments, ('mem', 'tile'), 0, 0, tiled=True, axis_index_...  9.08 us
    all_to_all x1, waiting for transfers between devices, body(): lax.all_to_all(smoothed, 'tile', 0, 0, tiled=True, axis_index_groups=by_c...  8.27 us
    all_to_all x1, starting transfers between devices, body(): lax.all_to_all(smoothed, 'tile', 0, 0, tiled=True, axis_index_groups=by_c...  7.53 us
    all_to_all x1, starting transfers between devices, body(): lax.all_to_all(fields, ('mem', 'tile'), 0, 0, tiled=True, axis_index_grou...  7.32 us
    ppermute x2, starting transfers between devices, body(): obs.append(lax.ppermute(seen[k], ('mem', 'tile'), targets))  6.74 us
    pallas_call x1, Pallas kernels, transform(): pl.pallas_call(transform_kernel, in_specs=[pl.BlockSpec(memory_space=pltp...  4.46 us
    ppermute x2, waiting for transfers between devices, body(): obs.append(lax.ppermute(seen[k], ('mem', 'tile'), targets))  1.96 us
  transfers between devices with their start and end apart: 4, of which 3 were waited for; matrix products, arithmetic and copies ran while one was open for 0% of the time, Pallas kernels for 2%

profile of v6, /device:TPU:1, one launch (start us, length us, event | category | flops | bytes accessed | tf_op | source)
XLA Modules:
  0.0 74.6 jit_solution(12722036617866550663)
XLA Ops:
  0.0 0.0 copy-start.1
  0.0 0.0 copy-start
  0.0 24.8 %forecast.1 = (bf16[16,72,128]{2,1,0:T(8,128)(2,1)}, f32[2,16,69]{2,1,0:T(8,128)}, f32[2,16,69]{2,1,0:T(8,128)}) custom-call(s32[1]{0:T(128)} %bitcast.1.place_ref, bf16[1024,1024]{1,0:T(8,128)(2,1)} %bitcast.5, bf16[1024]{0:T(1024)(128)(2,1)} %gain_ref.1, bf16[1024,4096]{1,0:T(8,128)(2,1)} %win_ref.1, bf16[4096,1024]{1,0:T(8,128)(2,1)} %wout_ref.1, ...), custom_call_target="tpu_custom_call" | custom-call | flops 17179869184 | bytes 16777216 | tf_op jit(solution)/shard_map/forecast/pallas_call | solution.py:156
  24.8 7.3 %all-to-all-start = ((bf16[16,72,128]{2,1,0:T(8,128)(2,1)}), bf16[16,72,128]{2,1,0:T(8,128)(2,1)S(1)}, u32[]{:S(2)}, u32[]{:S(2)}) async-start(bf16[16,72,128]{2,1,0:T(8,128)(2,1)} %get-tuple-element.12), calls=%async_computation | async-start | bytes 589824 | tf_op jit(solution)/shard_map/all_to_all | solution.py:561
  32.2 2.8 %collective-permute-start = (f32[2,16,69]{2,1,0:T(8,128)}, f32[2,16,69]{2,1,0:T(8,128)S(1)}, u32[]{:S(2)}, u32[]{:S(2)}) collective-permute-start(f32[2,16,69]{2,1,0:T(8,128)} %get-tuple-element.16), channel_id=1, source_target_pairs={{0,8},{1,9},{2,30},{3,31},{4,36},{5,37},{6,58},{7,59},{8,66},{9,67... | collective-permute-start | bytes 26504 | tf_op jit(solution)/shard_map/ppermute | solution.py:572
  34.9 4.0 %collective-permute-start.1 = (f32[2,16,69]{2,1,0:T(8,128)}, f32[2,16,69]{2,1,0:T(8,128)S(1)}, u32[]{:S(2)}, u32[]{:S(2)}) collective-permute-start(f32[2,16,69]{2,1,0:T(8,128)} %get-tuple-element.17), channel_id=1, source_target_pairs={{0,119},{1,8},{2,11},{3,30},{4,17},{5,36},{6,39},{7,58},{8,61},{9,... | collective-permute-start | bytes 26504 | tf_op jit(solution)/shard_map/ppermute | solution.py:572
  38.9 0.7 all-to-all-done.recv_ref
  39.6 0.0 copy-done.1
  39.6 1.6 %pairs.1 = (f32[144,256]{1,0:T(8,128)S(1)}, f32[2,8,72,128]{3,2,1,0:T(8,128)S(1)}, f32[2,72,128]{2,1,0:T(8,128)S(1)}, f32[8,72,128]{2,1,0:T(8,128)S(1)}) custom-call(bf16[16,72,128]{2,1,0:T(8,128)(2,1)S(1)} %all-to-all-done.recv_ref, f32[69]{0:T(128)S(1)} %copy-done.1), custom_call_target="tpu_custom_call" | custom-call | tf_op jit(solution)/shard_map/pairs/pallas_call | solution.py:309
  41.1 0.0 collective-permute-done.west_ref
  41.2 2.0 %collective-permute-done.1.east_ref = f32[2,16,69]{2,1,0:T(8,128)S(1)} collective-permute-done((f32[2,16,69]{2,1,0:T(8,128)}, f32[2,16,69]{2,1,0:T(8,128)S(1)}, u32[]{:S(2)}, u32[]{:S(2)}) %collective-permute-start.1) | collective-permute-done | bytes 8864 | tf_op jit(solution)/shard_map/ppermute | solution.py:572
  43.1 0.0 copy-done
  43.1 1.1 %smooth.1 = bf16[8,144,128]{2,1,0:T(8,128)(2,1)} custom-call(f32[144,256]{1,0:T(8,128)S(1)} %get-tuple-element.13.sums_ref, f32[2,8,72,128]{3,2,1,0:T(8,128)S(1)} %get-tuple-element.14.weighted, f32[2,72,128]{2,1,0:T(8,128)S(1)} %get-tuple-element.15.mean_ref, f32[2,16,69]{2,1,0:T(8,128)S(1)} %collective-permute-done.west_ref, ...), custom_call_target="tpu_custom_call" | custom-call | tf_op jit(solution)/shard_map/smooth/pallas_call | solution.py:330
  44.2 7.5 %all-to-all-start.1 = ((bf16[8,144,128]{2,1,0:T(8,128)(2,1)}), bf16[8,144,128]{2,1,0:T(8,128)(2,1)S(1)}, u32[]{:S(2)}, u32[]{:S(2)}) async-start(bf16[8,144,128]{2,1,0:T(8,128)(2,1)} %smooth.1), calls=%async_computation.1 | async-start | bytes 589824 | tf_op jit(solution)/shard_map/all_to_all | solution.py:576
  51.7 8.3 %all-to-all-done.1.recv_ref = bf16[8,144,128]{2,1,0:T(8,128)(2,1)S(1)} async-done(((bf16[8,144,128]{2,1,0:T(8,128)(2,1)}), bf16[8,144,128]{2,1,0:T(8,128)(2,1)S(1)}, u32[]{:S(2)}, u32[]{:S(2)}) %all-to-all-start.1) | async-done | bytes 294944 | tf_op jit(solution)/shard_map/all_to_all | solution.py:576
  60.0 4.5 %transform.1 = bf16[16,40,128]{2,1,0:T(8,128)(2,1)S(1)} custom-call(s32[1]{0:T(128)} %bitcast.place_ref, bf16[8,144,128]{2,1,0:T(8,128)(2,1)S(1)} %all-to-all-done.1.recv_ref, f32[8,72,128]{2,1,0:T(8,128)S(1)} %get-tuple-element.18.anom_ref), custom_call_target="tpu_custom_call" | custom-call | tf_op jit(solution)/shard_map/transform/pallas_call | solution.py:474
  64.4 9.1 %all_to_all.15.recv_ref = bf16[16,40,128]{2,1,0:T(8,128)(2,1)S(1)} all-to-all(bf16[16,40,128]{2,1,0:T(8,128)(2,1)S(1)} %transform.1), channel_id=1, replica_groups={{0,1,16,17,32,33,48,49,64,65,80,81,96,97,112,113},{2,3,18,19,34,35,50,5..., dimensions={0} | all-to-all | bytes 327680 | tf_op jit(solution)/shard_map/all_to_all | solution.py:578
  73.5 1.1 %strips.1 = f32[4,69,1,256]{3,2,1,0:T(1,128)} custom-call(bf16[16,40,128]{2,1,0:T(8,128)(2,1)S(1)} %all_to_all.15.recv_ref), custom_call_target="tpu_custom_call" | custom-call | tf_op jit(solution)/shard_map/strips/pallas_call | solution.py:526
Async XLA Ops:
  0.0 39.6 %copy-start.1 = (f32[69]{0:T(128)S(1)}, f32[69]{0:T(128)}, u32[]{:S(2)}) copy-start(f32[69]{0:T(128)} %err_ref.1) | copy-start | bytes 832
  0.0 43.1 %copy-start = (f32[256,128]{1,0:T(8,128)S(1)}, f32[256,128]{1,0:T(8,128)}, u32[]{:S(2)}) copy-start(f32[256,128]{1,0:T(8,128)} %constant.18.clone.taper_ref) | copy-start | bytes 393220
  24.8 14.7 %all-to-all-start = ((bf16[16,72,128]{2,1,0:T(8,128)(2,1)}), bf16[16,72,128]{2,1,0:T(8,128)(2,1)S(1)}, u32[]{:S(2)}, u32[]{:S(2)}) async-start(bf16[16,72,128]{2,1,0:T(8,128)(2,1)} %get-tuple-element.12), calls=%async_computation | async-start | bytes 589824 | tf_op jit(solution)/shard_map/all_to_all | solution.py:561
  32.2 9.0 %collective-permute-start = (f32[2,16,69]{2,1,0:T(8,128)}, f32[2,16,69]{2,1,0:T(8,128)S(1)}, u32[]{:S(2)}, u32[]{:S(2)}) collective-permute-start(f32[2,16,69]{2,1,0:T(8,128)} %get-tuple-element.16), channel_id=1, source_target_pairs={{0,8},{1,9},{2,30},{3,31},{4,36},{5,37},{6,58},{7,59},{8,66},{9,67... | collective-permute-start | bytes 26504 | tf_op jit(solution)/shard_map/ppermute | solution.py:572
  34.9 8.2 %collective-permute-start.1 = (f32[2,16,69]{2,1,0:T(8,128)}, f32[2,16,69]{2,1,0:T(8,128)S(1)}, u32[]{:S(2)}, u32[]{:S(2)}) collective-permute-start(f32[2,16,69]{2,1,0:T(8,128)} %get-tuple-element.17), channel_id=1, source_target_pairs={{0,119},{1,8},{2,11},{3,30},{4,17},{5,36},{6,39},{7,58},{8,61},{9,... | collective-permute-start | bytes 26504 | tf_op jit(solution)/shard_map/ppermute | solution.py:572
  44.2 15.8 %all-to-all-start.1 = ((bf16[8,144,128]{2,1,0:T(8,128)(2,1)}), bf16[8,144,128]{2,1,0:T(8,128)(2,1)S(1)}, u32[]{:S(2)}, u32[]{:S(2)}) async-start(bf16[8,144,128]{2,1,0:T(8,128)(2,1)} %smooth.1), calls=%async_computation.1 | async-start | bytes 589824 | tf_op jit(solution)/shard_map/all_to_all | solution.py:576
